TPU v7x, 32 devices: a whole 2x2x4 slice. The times are simulated.
32 devices in a mesh: groups: 2 (over x), tensor: 16 (over z, y, core).
Axes of the slice: x: 2, y: 2, z: 4, core: 2. Of those that a mesh axis runs over, the one named last changes fastest.
Arguments:
- mixer_in: bfloat16 [1024, 4096], P('groups', 'tensor'), parts along dimension 0, may hold values from -6 to 6
- gate_in: bfloat16 [1024, 4096], P('groups', 'tensor'), parts along dimension 0, may hold values from -6 to 6
- conv_tail: bfloat16 [3, 256, 4096], P(None, 'groups', 'tensor'), parts along dimension 1, may hold values from -6 to 6
- ssm_state: bfloat16 [256, 16, 4096], P('groups', None, 'tensor'), parts along dimension 0, may hold values from -6 to 6
- resid: bfloat16 [1024, 8192], P(('groups', 'tensor')), parts along dimension 0, may hold values from -6 to 6
- expert_ids: int32 [1024, 2], P('groups'), parts along dimension 0, may hold values from 0 to 15, as said below
- conv_weight: bfloat16 [4, 4096], P(None, 'tensor'), may hold values from -3 to 3
- conv_bias: float32 [4096], P('tensor'), may hold values from -3 to 3
- x_weight: bfloat16 [4096, 544], P('tensor'), may hold values from -0.09375 to 0.09375
- dt_weight: bfloat16 [512, 4096], P(None, 'tensor'), may hold values from -0.25 to 0.25
- dt_bias: float32 [4096], P('tensor'), may hold values from -4 to -1
- decay_log: float32 [16, 4096], P(None, 'tensor'), may hold values from -1 to 2.5
- skip_gain: float32 [4096], P('tensor'), may hold values from 0.5 to 1.5
- out_weight: bfloat16 [4096, 8192], P('tensor'), may hold values from -0.09375 to 0.09375
- norm_gain: bfloat16 [8192], replicated, may hold values from 0.5 to 2
- router_weight: bfloat16 [8192, 16], replicated, may hold values from -0.0625 to 0.0625
- w_gate: bfloat16 [8192, 6144], P(None, 'tensor'), may hold values from -0.0625 to 0.0625
- w_up: bfloat16 [8192, 6144], P(None, 'tensor'), may hold values from -0.0625 to 0.0625
- w_down: bfloat16 [6144, 8192], P('tensor'), may hold values from -0.078125 to 0.078125
Outputs:
- layer_out: bfloat16 [1024, 8192], P(('groups', 'tensor')), parts along dimension 0
- state_out: bfloat16 [256, 16, 4096], P('groups', None, 'tensor'), parts along dimension 0
There are 2 independent parts, one for each index of `groups`. A program takes and returns all parts, laid end to end along the dimension named above; an argument that names none is the same for every part. Nothing has to cross between parts.
Inputs may be any that keep to these rules, and one draw needn't show every extreme that they name: `expert_ids`: the two ids of a token differ. In each aligned block of 32 tokens at least one and at most 12 tokens name expert 0, and in some block exactly 12 do.
All inputs are finite; a program needn't handle non-finite values.
Results may differ from a plain program's by a relative error of at most 0.023.
Values may be sent and summed in bfloat16 or wider, within the bound.
A program may use at most 192 MiB of HBM per device.

v0:
```python
import jax
import jax.numpy as jnp
from jax import lax
from jax.sharding import PartitionSpec as P

RANK = 512
STATE = 16
CONV = 4
EXPERTS = 16
TOPK = 2
STEPS = 4
REQ = 128


EPSILON = 1e-06


def convolve(mixer_in, conv_tail, conv_weight, conv_bias):
    width = mixer_in.shape[1]
    inputs = mixer_in.reshape(STEPS, REQ, width).astype(jnp.float32)
    history = jnp.concatenate([conv_tail.astype(jnp.float32), inputs], axis=0)
    kernel = conv_weight.astype(jnp.float32)
    summed = conv_bias[None, None, :] + kernel[0] * history[0:STEPS]
    for offset in range(1, CONV):
        summed = summed + kernel[offset] * history[offset : offset + STEPS]
    return jax.nn.silu(summed).astype(jnp.bfloat16).reshape(STEPS * REQ, width)


def run_states(mixed, gate_in, delta, b_part, c_part, ssm_state, decay_log, skip_gain):
    rate = -jnp.exp(decay_log)
    state = ssm_state.astype(jnp.float32)
    results = []
    for position in range(STEPS):
        first = position * REQ
        step_delta = delta[first : first + REQ]
        step_input = mixed[first : first + REQ].astype(jnp.float32)
        decay = jnp.exp(step_delta[:, None, :] * rate[None, :, :])
        state = (
            decay * state
            + (step_delta * step_input)[:, None, :] * b_part[first : first + REQ][:, :, None]
        )
        reading = (
            jnp.sum(c_part[first : first + REQ][:, :, None] * state, axis=1)
            + skip_gain[None, :] * step_input
        )
        results.append(reading * jax.nn.silu(gate_in[first : first + REQ].astype(jnp.float32)))
    return (jnp.concatenate(results, axis=0).astype(jnp.bfloat16), state.astype(jnp.bfloat16))


def route_inputs(hidden_state, expert_ids, norm_gain, router_weight):
    scale = lax.rsqrt(jnp.mean(hidden_state * hidden_state, axis=1, keepdims=True) + EPSILON)
    normed = (hidden_state * scale * norm_gain.astype(jnp.float32)[None, :]).astype(jnp.bfloat16)
    logits = jnp.dot(normed, router_weight, preferred_element_type=jnp.float32)
    labels = jnp.arange(logits.shape[1], dtype=jnp.int32)
    onehot = expert_ids[:, :, None] == labels[None, None, :]
    picked = jnp.sum(jnp.where(onehot, logits[:, None, :], 0.0), axis=2)
    weight_first = jax.nn.sigmoid(picked[:, 0] - picked[:, 1])
    weight_second = jax.nn.sigmoid(picked[:, 1] - picked[:, 0])
    route_weight = jnp.where(
        expert_ids[:, 0] == 0, weight_first, jnp.where(expert_ids[:, 1] == 0, weight_second, 0.0)
    )
    return (normed, route_weight)


def slot_matrix(own_ids, route_weight, most):
    member = jnp.logical_or(own_ids[:, 0] == 0, own_ids[:, 1] == 0).astype(jnp.int32)
    ranked = jnp.cumsum(member, dtype=jnp.int32) - member
    slots = jnp.arange(most, dtype=jnp.int32)
    choose = jnp.logical_and(member[None, :] > 0, ranked[None, :] == slots[:, None])
    choose_real = choose.astype(jnp.float32)
    return (choose_real, choose_real * route_weight[None, :])


def expert_hidden_rows(rows, w_gate, w_up):
    gated = jnp.dot(rows, w_gate, preferred_element_type=jnp.float32)
    upward = jnp.dot(rows, w_up, preferred_element_type=jnp.float32)
    return (jax.nn.silu(gated) * upward).astype(jnp.bfloat16)


def per_device(
    mixer_in,
    gate_in,
    conv_tail,
    ssm_state,
    resid,
    expert_ids,
    conv_weight,
    conv_bias,
    x_weight,
    dt_weight,
    dt_bias,
    decay_log,
    skip_gain,
    out_weight,
    norm_gain,
    router_weight,
    w_gate,
    w_up,
    w_down,
):
    devices = lax.axis_size("tensor")
    tokens_total = mixer_in.shape[0]
    own_count = tokens_total // devices
    most = max(2, own_count * TOPK * 3 // EXPERTS)
    mixed = convolve(mixer_in, conv_tail, conv_weight, conv_bias)
    partial_proj = jnp.dot(mixed, x_weight, preferred_element_type=jnp.float32)
    projected = lax.psum(partial_proj.astype(jnp.bfloat16), "tensor").astype(jnp.float32)
    rank_part = projected[:, :RANK].astype(jnp.bfloat16)
    delta = jax.nn.softplus(
        jnp.dot(rank_part, dt_weight, preferred_element_type=jnp.float32) + dt_bias[None, :]
    )
    b_part = projected[:, RANK : RANK + STATE]
    c_part = projected[:, RANK + STATE :]
    readout, state_out = run_states(
        mixed, gate_in, delta, b_part, c_part, ssm_state, decay_log, skip_gain
    )
    position = lax.axis_index("tensor")
    piece = readout
    mixer_rows = lax.psum_scatter(
        jnp.dot(piece, out_weight, preferred_element_type=jnp.float32).astype(jnp.bfloat16),
        "tensor",
        scatter_dimension=0,
        tiled=True,
    ).astype(jnp.float32)
    own_ids = lax.dynamic_slice_in_dim(expert_ids, position * own_count, own_count, 0)
    hidden_state = resid.astype(jnp.float32) + mixer_rows
    normed, route_weight = route_inputs(hidden_state, own_ids, norm_gain, router_weight)
    choose_real, coefficient = slot_matrix(own_ids, route_weight, most)
    packed = jnp.dot(
        choose_real.astype(jnp.bfloat16), normed, preferred_element_type=jnp.float32
    ).astype(jnp.bfloat16)
    all_hidden = expert_hidden_rows(
        lax.all_gather(packed, "tensor", axis=0, tiled=True), w_gate, w_up
    )
    piece = all_hidden
    summed = lax.psum_scatter(
        jnp.dot(piece, w_down, preferred_element_type=jnp.float32)
        .astype(jnp.bfloat16)
        .astype(jnp.float32)
        .astype(jnp.bfloat16),
        "tensor",
        scatter_dimension=0,
        tiled=True,
    ).astype(jnp.float32)
    expert_rows = jnp.dot(coefficient.T, summed, precision=lax.Precision.HIGHEST)
    layer_out = (hidden_state + expert_rows).astype(jnp.bfloat16)
    return (layer_out, state_out)


def solution(mesh):
    return jax.shard_map(
        per_device,
        mesh=mesh,
        in_specs=(
            P("groups", "tensor"),
            P("groups", "tensor"),
            P(None, "groups", "tensor"),
            P("groups", None, "tensor"),
            P(("groups", "tensor"), None),
            P("groups", None),
            P(None, "tensor"),
            P("tensor"),
            P("tensor", None),
            P(None, "tensor"),
            P("tensor"),
            P(None, "tensor"),
            P("tensor"),
            P("tensor", None),
            P(),
            P(),
            P(None, "tensor"),
            P(None, "tensor"),
            P("tensor", None),
        ),
        out_specs=(P(("groups", "tensor"), None), P("groups", None, "tensor")),
        check_vma=False,
    )
```

profile of v0, /device:TPU:0, one launch (start us, length us, event | category | flops | bytes accessed | tf_op | source)
XLA Modules:
  0.0 381.7 jit_solution(2358190996203299171)
XLA Ops:
  7.2 0.8 fusion.71
  8.1 1.0 convert.22
  9.1 1.0 convert_element_type.116
  10.1 0.9 multiply_convert_fusion.1
  11.0 1.1 convolution_convert_fusion.3
  12.3 93.3 %all-reduce.4.cloned.1.call-done = bf16[512,544]{0,1:T(8,128)(2,1)} async-done(((bf16[512,544]{0,1:T(8,128)(2,1)}), bf16[512,544]{0,1:T(8,128)(2,1)}) %all-reduce.4.cloned.1.call-update) | async-done | bytes 557072 | tf_op jit(solution)/shard_map/psum | solution.py:107
  105.6 1.6 compare_select_fusion
  107.3 0.7 fusion.70
  108.9 5.0 %multiply_reduce_fusion.1 = (f32[128,256]{1,0:T(8,128)S(1)}, f32[128,256]{1,0:T(8,128)S(1)}, f32[128,256]{1,0:T(8,128)S(1)}, f32[128,256]{1,0:T(8,128)S(1)}, bf16[128,16,256]{2,1,0:T(8,128)(2,1)}) fusion(f32[128,16]{1,0:T(8,128)S(1)} %copy.59, f32[128,256]{1,0:T(8,128)S(1)} %get-tuple-element.8, f32[128,256]{1,0:T(8,128)S(1)} %get-tuple-element.24, ...), kind=kLoop, calls=%fused_computation.8 | loop fusion | flops 13500416 | bytes 3751936 | tf_op jit(solution)/shard_map/reduce_sum | solution.py:43
  113.9 0.2 fusion.54
  114.1 5.6 %convolution_convert_fusion = bf16[512,8192]{1,0:T(8,128)(2,1)} fusion(bf16[256,8192]{1,0:T(8,128)(2,1)S(1)} %copy-done.3, bf16[128,256]{1,0:T(8,128)(2,1)S(1)} %get-tuple-element.21, bf16[128,256]{1,0:T(8,128)(2,1)S(1)} %get-tuple-element.22, bf16[128,256]{1,0:T(8,128)(2,1)S(1)} %get-tuple-element.20, bf16[128,256]{1,0:T(8,128)(2,1)S(1)} %get-tuple-element.19), kind=kOutput, calls=%fused_computation | convolution fusion | flops 2152726528 | bytes 12845056 | tf_op jit(solution)/shard_map/dot_general | solution.py:120
  119.8 0.6 copy-done.8
  120.4 0.7 constant_dynamic-slice_fusion
  121.4 102.9 %reduce-scatter.4.cloned.1.call-done = bf16[32,8192]{1,0:T(8,128)(2,1)} async-done(((bf16[512,8192]{1,0:T(8,128)(2,1)}), bf16[32,8192]{1,0:T(8,128)(2,1)}) %reduce-scatter.4.cloned.1.call-update) | async-done | bytes 524304 | tf_op jit(solution)/shard_map/reduce_scatter | solution.py:119
  224.3 1.3 multiply_reduce_fusion.4
  225.6 1.2 multiply_convert_fusion
  226.9 0.9 fusion.2
  227.8 0.6 dynamic-slice.4
  229.1 0.2 fusion.72
  229.3 49.0 %all-gather.3.cloned.1.call-done = bf16[16,12,8192]{2,1,0:T(8,128)(2,1)} async-done(((bf16[1,12,8192]{2,1,0:T(8,128)(2,1)}), bf16[16,12,8192]{2,1,0:T(8,128)(2,1)}) %all-gather.3.cloned.1.call-update) | async-done | bytes 3145744 | tf_op jit(solution)/shard_map/all_gather | solution.py:133
  278.3 4.7 %reshape.157 = bf16[192,8192]{1,0:T(8,128)(2,1)} reshape(bf16[16,12,8192]{2,1,0:T(8,128)(2,1)} %all-gather.3.cloned.1.call-done) | data formatting | bytes 6291456
  283.0 5.5 %fusion.73 = f32[192,384]{1,0:T(8,128)S(1)} fusion(bf16[192,8192]{1,0:T(8,128)(2,1)} %reshape.157, bf16[8192,384]{1,0:T(8,128)(2,1)} %param.35), kind=kOutput, calls=%fused_computation.128 | convolution fusion | flops 1207959552 | bytes 9732096 | tf_op jit(solution)/shard_map/dot_general | solution.py:75
  288.6 10.7 %convolution_convert_fusion.1 = bf16[192,8192]{1,0:T(8,128)(2,1)} fusion(bf16[384,8192]{1,0:T(8,128)(2,1)} %param.37, bf16[192,8192]{1,0:T(8,128)(2,1)} %reshape.157, bf16[8192,384]{1,0:T(8,128)(2,1)} %param.36, f32[192,384]{1,0:T(8,128)S(1)} %fusion.73), kind=kOutput, calls=%fused_computation.1 | convolution fusion | flops 2417934336 | bytes 19169280 | tf_op jit(solution)/shard_map/dot_general | solution.py:137
  299.3 48.5 %fusion = bf16[16,8192]{1,0:T(8,128)(2,1)S(1)} fusion(bf16[192,8192]{1,0:T(8,128)(2,1)} %convolution_convert_fusion.1), kind=kCustom, calls=%all-reduce-scatter | all-reduce-scatter fusion | flops 2097153 | bytes 3408384
  347.8 4.3 %collective-permute-start = (bf16[16,8192]{1,0:T(8,128)(2,1)S(1)}, bf16[16,8192]{1,0:T(8,128)(2,1)S(1)}, u32[]{:S(2)}, u32[]{:S(2)}) collective-permute-start(bf16[16,8192]{1,0:T(8,128)(2,1)S(1)} %fusion), channel_id=1, source_target_pairs={{0,1},{1,2},{2,3},{3,4},{4,5},{5,6},{6,7},{7,8},{8,9},{9,10},{10,1... | collective-permute-start | bytes 786440
  352.1 4.2 %collective-permute-start.1 = (bf16[16,8192]{1,0:T(8,128)(2,1)S(1)}, bf16[16,8192]{1,0:T(8,128)(2,1)S(1)}, u32[]{:S(2)}, u32[]{:S(2)}) collective-permute-start(bf16[16,8192]{1,0:T(8,128)(2,1)S(1)} %fusion), channel_id=1, source_target_pairs={{0,2},{1,3},{2,4},{3,5},{4,6},{5,7},{6,8},{7,9},{8,10},{9,11},{10,... | collective-permute-start | bytes 786440
  356.3 3.0 collective-permute-start.2
  359.4 2.9 collective-permute-start.3
  362.3 4.9 %collective-permute-done.3 = bf16[12,8192]{1,0:T(8,128)(2,1)S(1)} collective-permute-done((bf16[12,8192]{1,0:T(8,128)(2,1)S(1)}, bf16[12,8192]{1,0:T(8,128)(2,1)S(1)}, u32[]{:S(2)}, u32[]{:S(2)}) %collective-permute-start.3) | collective-permute-done | bytes 196640
  367.2 0.7 copy-done.6
  367.9 5.7 %concatenate.9 = bf16[76,8192]{1,0:T(8,128)(2,1)S(1)} concatenate(bf16[12,8192]{1,0:T(8,128)(2,1)} %copy-done.6, bf16[16,8192]{1,0:T(8,128)(2,1)} %collective-permute-done.2, bf16[16,8192]{1,0:T(8,128)(2,1)S(1)} %collective-permute-done.1, bf16[16,8192]{1,0:T(8,128)(2,1)S(1)} %collective-permute-done, bf16[16,8192]{1,0:T(8,128)(2,1)S(1)} %fusion), dimensions={0} | concatenate | bytes 2490368
  373.7 1.5 fusion.1
  (56 shorter events, 1.5 us)
Async XLA Ops:
  7.2 3.8 %copy-start = (bf16[256,544]{0,1:T(8,128)(2,1)S(1)}, bf16[256,544]{0,1:T(8,128)(2,1)}, u32[]{:S(2)}) copy-start(bf16[256,544]{0,1:T(8,128)(2,1)} %param.27) | copy-start | bytes 835588
  7.2 98.5 %all-reduce.4.cloned.1.call-start = ((), (), s32[]{:S(2)}) async-start(), calls=%async_computation.1 | async-start | bytes 1114112 | tf_op jit(solution)/shard_map/psum | solution.py:107
  8.1 4.2 %copy-start.9 = (f32[16,256]{1,0:T(8,128)S(1)}, f32[16,256]{1,0:T(8,128)}, u32[]{:S(2)}) copy-start(f32[16,256]{1,0:T(8,128)} %param.30) | copy-start | bytes 49156
  8.1 97.6 %copy-start.12 = (bf16[512,256]{1,0:T(8,128)(2,1)S(1)}, bf16[512,256]{1,0:T(8,128)(2,1)}, u32[]{:S(2)}) copy-start(bf16[512,256]{1,0:T(8,128)(2,1)} %param.28) | copy-start | bytes 786436
  8.1 97.6 %copy-start.13 = (f32[256]{0:T(256)S(1)}, f32[256]{0:T(256)}, u32[]{:S(2)}) copy-start(f32[256]{0:T(256)} %param.29) | copy-start | bytes 3076
  12.2 212.1 %reduce-scatter.4.cloned.1.call-start = ((), (), s32[]{:S(2)}) async-start(), calls=%async_computation.2 | async-start | bytes 8912896 | tf_op jit(solution)/shard_map/reduce_scatter | solution.py:119
  12.3 96.6 %copy-start.4 = (bf16[128,16,256]{2,1,0:T(8,128)(2,1)S(1)}, bf16[128,16,256]{2,1,0:T(8,128)(2,1)}, u32[]{:S(2)}) copy-start(bf16[128,16,256]{2,1,0:T(8,128)(2,1)} %param.22) | copy-start | bytes 3145732
  108.6 5.2 %copy-start.7 = (bf16[512,256]{1,0:T(8,128)(2,1)S(1)}, bf16[512,256]{1,0:T(8,128)(2,1)}, u32[]{:S(2)}) copy-start(bf16[512,256]{1,0:T(8,128)(2,1)} %param.20) | copy-start | bytes 786436
  108.6 5.2 %copy-start.10 = (f32[256]{0:T(256)S(1)}, f32[256]{0:T(256)}, u32[]{:S(2)}) copy-start(f32[256]{0:T(256)} %param.31) | copy-start | bytes 3076
  108.9 5.2 %copy-start.3 = (bf16[256,8192]{1,0:T(8,128)(2,1)S(1)}, bf16[256,8192]{1,0:T(8,128)(2,1)}, u32[]{:S(2)}) copy-start(bf16[256,8192]{1,0:T(8,128)(2,1)} %param.32) | copy-start | bytes 12582916
  119.7 0.7 copy-start.8
  119.7 104.7 %copy-start.1 = (bf16[32,8192]{1,0:T(8,128)(2,1)S(1)}, bf16[32,8192]{1,0:T(8,128)(2,1)}, u32[]{:S(2)}) copy-start(bf16[32,8192]{1,0:T(8,128)(2,1)} %param.23) | copy-start | bytes 1572868
  119.7 108.2 %copy-start.11 = (u32[32]{0:T(128)S(1)}, u32[32]{0:T(128)}, u32[]{:S(2)}) copy-start(u32[32]{0:T(128)} %constant.38) | copy-start | bytes 388
  119.7 109.4 %copy-start.5 = (bf16[8192,16]{0,1:T(8,128)(2,1)S(1)}, bf16[8192,16]{0,1:T(8,128)(2,1)}, u32[]{:S(2)}) copy-start(bf16[8192,16]{0,1:T(8,128)(2,1)} %param.34) | copy-start | bytes 786436
  119.7 158.6 %all-gather.3.cloned.1.call-start = ((), (), s32[]{:S(2)}) async-start(), calls=%async_computation.3 | async-start | bytes 4456448 | tf_op jit(solution)/shard_map/all_gather | solution.py:133
  347.8 25.9 %copy-start.2 = (bf16[32,8192]{1,0:T(8,128)(2,1)S(1)}, bf16[32,8192]{1,0:T(8,128)(2,1)}, u32[]{:S(2)}) copy-start(bf16[32,8192]{1,0:T(8,128)(2,1)} %reduce-scatter.4.cloned.1.call-done) | copy-start | bytes 1572868
  347.8 19.4 %collective-permute-start = (bf16[16,8192]{1,0:T(8,128)(2,1)S(1)}, bf16[16,8192]{1,0:T(8,128)(2,1)S(1)}, u32[]{:S(2)}, u32[]{:S(2)}) collective-permute-start(bf16[16,8192]{1,0:T(8,128)(2,1)S(1)} %fusion), channel_id=1, source_target_pairs={{0,1},{1,2},{2,3},{3,4},{4,5},{5,6},{6,7},{7,8},{8,9},{9,10},{10,1... | collective-permute-start | bytes 786440
  352.1 15.1 %collective-permute-start.1 = (bf16[16,8192]{1,0:T(8,128)(2,1)S(1)}, bf16[16,8192]{1,0:T(8,128)(2,1)S(1)}, u32[]{:S(2)}, u32[]{:S(2)}) collective-permute-start(bf16[16,8192]{1,0:T(8,128)(2,1)S(1)} %fusion), channel_id=1, source_target_pairs={{0,2},{1,3},{2,4},{3,5},{4,6},{5,7},{6,8},{7,9},{8,10},{9,11},{10,... | collective-permute-start | bytes 786440
  356.3 11.6 %collective-permute-start.2 = (bf16[16,8192]{1,0:T(8,128)(2,1)S(1)}, bf16[16,8192]{1,0:T(8,128)(2,1)}, u32[]{:S(2)}, u32[]{:S(2)}) collective-permute-start(bf16[16,8192]{1,0:T(8,128)(2,1)S(1)} %fusion), channel_id=1, source_target_pairs={{0,3},{1,4},{2,5},{3,6},{4,7},{5,8},{6,9},{7,10},{8,11},{9,12},{10... | collective-permute-start | bytes 786440
  359.4 7.8 %collective-permute-start.3 = (bf16[12,8192]{1,0:T(8,128)(2,1)S(1)}, bf16[12,8192]{1,0:T(8,128)(2,1)S(1)}, u32[]{:S(2)}, u32[]{:S(2)}) collective-permute-start(bf16[12,8192]{1,0:T(8,128)(2,1)S(1)} %slice.172), channel_id=1, source_target_pairs={{0,4},{1,5},{2,6},{3,7},{4,8},{5,9},{6,10},{7,11},{8,12},{9,13},{1... | collective-permute-start | bytes 589832
  367.2 0.7 copy-start.6
Sparse Core Ops, SparseCore 0:
  12.3 93.2 all-reduce.3
  119.8 104.4 reduce-scatter.3
  228.0 50.3 all-gather.2
where the time goes:
time: 388 us; the launch traced here: 382 us
  waiting for transfers between devices  250 us (64%)
  blocking collectives  48.5 us (12%)
  matrix products  27.2 us (7%)
  local copies, waits for them, and re-layouts  15.7 us (4%)
  between operations  14.6 us (4%)
  starting transfers between devices  14.5 us (4%)
  other arithmetic  11 us (3%)
    reduce_scatter x1, waiting for transfers between devices, per_device(): lax.psum_scatter(jnp.dot(piece, out_weight, preferred_element_type=jnp.fl...  103 us
    psum x1, waiting for transfers between devices, per_device(): lax.psum(partial_proj.astype(jnp.bfloat16), 'tensor').astype(jnp.float32)  93.3 us
    all_gather x1, waiting for transfers between devices, per_device(): lax.all_gather(packed, 'tensor', axis=0, tiled=True)  49 us
    unnamed x1, blocking collectives  48.5 us
    unnamed x4, starting transfers between devices  14.4 us
    unnamed x32, local copies, waits for them, and re-layouts  12.5 us
    dot_general x1, matrix products, per_device(): jnp.dot(piece, w_down, preferred_element_type=jnp.float32)  10.7 us
  transfers between devices with their start and end apart: 7, of which 4 were waited for; matrix products, arithmetic and copies ran while one was open for 1% of the time, Pallas kernels for 0%

commit v1 on v0

--- a/solution.py
+++ b/solution.py
@@ -1,6 +1,8 @@
 import jax
 import jax.numpy as jnp
 from jax import lax
+from jax.experimental import pallas as pl
+from jax.experimental.pallas import tpu as pltpu
 from jax.sharding import PartitionSpec as P
 
 RANK = 512
@@ -13,6 +15,287 @@
 
 
 EPSILON = 1e-06
+MESH = pl.DeviceIdType.MESH
+
+
+def radices(devices):
+    chips = devices // 2
+    outer = min(4, chips)
+    return (outer, chips // outer, 2)
+
+
+class Place:
+    def __init__(self, devices):
+        self.d2, self.d1, self.d0 = radices(devices)
+        self.group = lax.axis_index("groups")
+        me = lax.axis_index("tensor")
+        self.i0 = lax.rem(me, self.d0)
+        self.i1 = lax.rem(me // self.d0, self.d1)
+        self.i2 = me // (self.d0 * self.d1)
+
+    def digit(self, stage, step):
+        now = (self.i0, self.i1, self.i2)[stage]
+        radix = (self.d0, self.d1, self.d2)[stage]
+        return lax.rem(now + step, radix)
+
+    def device(self, stage, step):
+        index = [self.i0, self.i1, self.i2]
+        index[stage] = self.digit(stage, step)
+        return (self.group, (index[2] * self.d1 + index[1]) * self.d0 + index[0])
+
+    def barrier(self):
+        semaphore = pltpu.get_barrier_semaphore()
+        count = 0
+        for stage, radix in enumerate((self.d0, self.d1, self.d2)):
+            for step in range(1, radix):
+                pl.semaphore_signal(
+                    semaphore, inc=1, device_id=self.device(stage, step), device_id_type=MESH
+                )
+                count += 1
+        pl.semaphore_wait(semaphore, count)
+
+
+def send(source, target, send_sem, recv_sem, device):
+    copy = pltpu.make_async_remote_copy(
+        src_ref=source,
+        dst_ref=target,
+        send_sem=send_sem,
+        recv_sem=recv_sem,
+        device_id=device,
+        device_id_type=MESH,
+    )
+    copy.start()
+    return copy
+
+
+def real(value):
+    return value.astype(jnp.float32)
+
+
+def reduce_parts(place, chunks, x_ref, finish, recv0, recv1, recv2, sems):
+    d2, d1, d0 = place.d2, place.d1, place.d0
+    width = x_ref.shape[-1] // chunks
+    copies = []
+
+    def columns(chunk):
+        return slice(None) if chunks == 1 else pl.ds(chunk * width, width)
+
+    def start0(chunk):
+        return [
+            send(
+                x_ref.at[:, :, place.digit(0, step), :, columns(chunk)],
+                recv0.at[chunk, step - 1],
+                sems[0].at[chunk, step - 1],
+                sems[1].at[chunk, step - 1],
+                place.device(0, step),
+            )
+            for step in range(1, d0)
+        ]
+
+    def start1(chunk):
+        def add(outer, carry):
+            for inner in range(d1):
+                total = real(x_ref[outer, inner, place.i0, :, columns(chunk)])
+                for step in range(1, d0):
+                    total = total + real(recv0[chunk, step - 1, outer, inner])
+                recv0[chunk, 0, outer, inner] = total.astype(recv0.dtype)
+            return carry
+
+        lax.fori_loop(0, d2, add, 0)
+        return [
+            send(
+                recv0.at[chunk, 0, :, place.digit(1, step)],
+                recv1.at[chunk, step - 1],
+                sems[2].at[chunk, step - 1],
+                sems[3].at[chunk, step - 1],
+                place.device(1, step),
+            )
+            for step in range(1, d1)
+        ]
+
+    def start2(chunk):
+        def add(outer, carry):
+            total = real(recv0[chunk, 0, outer, place.i1])
+            for step in range(1, d1):
+                total = total + real(recv1[chunk, step - 1, outer])
+            recv1[chunk, 0, outer] = total.astype(recv1.dtype)
+            return carry
+
+        lax.fori_loop(0, d2, add, 0)
+        return [
+            send(
+                recv1.at[chunk, 0, place.digit(2, step)],
+                recv2.at[chunk, step - 1],
+                sems[4].at[chunk, step - 1],
+                sems[5].at[chunk, step - 1],
+                place.device(2, step),
+            )
+            for step in range(1, d2)
+        ]
+
+    def last(chunk):
+        total = real(recv1[chunk, 0, place.i2])
+        for step in range(1, d2):
+            total = total + real(recv2[chunk, step - 1])
+        finish(chunk, columns(chunk), total)
+        return []
+
+    flying = {}
+    for tick in range(chunks + 3):
+        for stage, run in enumerate((start0, start1, start2, last)):
+            chunk = tick - stage
+            if 0 <= chunk < chunks:
+                if stage:
+                    for copy in flying[stage - 1, chunk]:
+                        copy.wait_recv()
+                flying[stage, chunk] = run(chunk)
+                copies.extend(flying[stage, chunk])
+    return copies
+
+
+def gather_parts(place, chunks, out_ref, sems):
+    d2, d1, d0 = place.d2, place.d1, place.d0
+    width = out_ref.shape[-1] // chunks
+    copies = []
+
+    def columns(chunk):
+        return slice(None) if chunks == 1 else pl.ds(chunk * width, width)
+
+    def held(stage, chunk):
+        if stage == 2:
+            return out_ref.at[place.i2, place.i1, place.i0, :, columns(chunk)]
+        if stage == 1:
+            return out_ref.at[:, place.i1, place.i0, :, columns(chunk)]
+        return out_ref.at[:, :, place.i0, :, columns(chunk)]
+
+    order = ((2, d2), (1, d1), (0, d0))
+    flying = {}
+    for tick in range(chunks + len(order)):
+        for spot in range(len(order) + 1):
+            chunk = tick - spot
+            if not 0 <= chunk < chunks:
+                continue
+            if spot:
+                for copy in flying[spot - 1, chunk]:
+                    copy.wait_recv()
+            if spot < len(order):
+                stage, radix = order[spot]
+                flying[spot, chunk] = [
+                    send(
+                        held(stage, chunk),
+                        held(stage, chunk),
+                        sems[2 * stage].at[chunk, step - 1],
+                        sems[2 * stage + 1].at[chunk, step - 1],
+                        place.device(stage, step),
+                    )
+                    for step in range(1, radix)
+                ]
+                copies.extend(flying[spot, chunk])
+    return copies
+
+
+def sem_shapes(devices, chunks):
+    d2, d1, d0 = radices(devices)
+    shapes = []
+    for radix in (d0, d1, d2):
+        shapes += [pltpu.SemaphoreType.DMA((chunks, max(1, radix - 1)))] * 2
+    return shapes
+
+
+def recv_shapes(devices, chunks, rows, width):
+    d2, d1, d0 = radices(devices)
+    return [
+        pltpu.VMEM((chunks, d0 - 1, d2, d1, rows, width), jnp.bfloat16),
+        pltpu.VMEM((chunks, max(1, d1 - 1), d2, rows, width), jnp.bfloat16),
+        pltpu.VMEM((chunks, max(1, d2 - 1), rows, width), jnp.bfloat16),
+    ]
+
+
+def params(number):
+    return pltpu.CompilerParams(
+        collective_id=number, has_side_effects=True, vmem_limit_bytes=56 * 1024 * 1024
+    )
+
+
+VMEM = pl.BlockSpec(memory_space=pltpu.VMEM)
+
+
+def all_sum(x, devices, number):
+    d2, d1, d0 = radices(devices)
+    rows, width = x.shape[0] // devices, x.shape[1]
+
+    def kernel(x_ref, out_ref, recv0, recv1, recv2, *sems):
+        place = Place(devices)
+        place.barrier()
+
+        def finish(chunk, columns, total):
+            out_ref[place.i2, place.i1, place.i0] = total.astype(out_ref.dtype)
+
+        copies = reduce_parts(place, 1, x_ref, finish, recv0, recv1, recv2, sems[:6])
+        copies += gather_parts(place, 1, out_ref, sems[6:])
+        for copy in copies:
+            copy.wait_send()
+
+    out = pl.pallas_call(
+        kernel,
+        out_shape=jax.ShapeDtypeStruct((d2, d1, d0, rows, width), jnp.bfloat16),
+        in_specs=[VMEM],
+        out_specs=VMEM,
+        scratch_shapes=recv_shapes(devices, 1, rows, width) + sem_shapes(devices, 1) * 2,
+        compiler_params=params(number),
+        name="all_sum",
+    )(x.reshape(d2, d1, d0, rows, width))
+    return out.reshape(x.shape)
+
+
+def scatter_sum(x, devices, chunks, number):
+    d2, d1, d0 = radices(devices)
+    rows, width = x.shape[0] // devices, x.shape[1]
+
+    def kernel(x_ref, out_ref, recv0, recv1, recv2, *sems):
+        place = Place(devices)
+        place.barrier()
+
+        def finish(chunk, columns, total):
+            out_ref[:, columns] = total
+
+        copies = reduce_parts(place, chunks, x_ref, finish, recv0, recv1, recv2, sems)
+        for copy in copies:
+            copy.wait_send()
+
+    return pl.pallas_call(
+        kernel,
+        out_shape=jax.ShapeDtypeStruct((rows, width), jnp.float32),
+        in_specs=[VMEM],
+        out_specs=VMEM,
+        scratch_shapes=recv_shapes(devices, chunks, rows, width // chunks)
+        + sem_shapes(devices, chunks),
+        compiler_params=params(number),
+        name="scatter_sum",
+    )(x.reshape(d2, d1, d0, rows, width))
+
+
+def gather(x, devices, chunks, number):
+    d2, d1, d0 = radices(devices)
+    rows, width = x.shape
+
+    def kernel(x_ref, out_ref, *sems):
+        place = Place(devices)
+        out_ref[place.i2, place.i1, place.i0] = x_ref[...]
+        place.barrier()
+        for copy in gather_parts(place, chunks, out_ref, sems):
+            copy.wait_send()
+
+    out = pl.pallas_call(
+        kernel,
+        out_shape=jax.ShapeDtypeStruct((d2, d1, d0, rows, width), x.dtype),
+        in_specs=[VMEM],
+        out_specs=VMEM,
+        scratch_shapes=sem_shapes(devices, chunks),
+        compiler_params=params(number),
+        name="gather",
+    )(x)
+    return out.reshape(devices * rows, width)
 
 
 def convolve(mixer_in, conv_tail, conv_weight, conv_bias):
@@ -102,9 +385,10 @@
     tokens_total = mixer_in.shape[0]
     own_count = tokens_total // devices
     most = max(2, own_count * TOPK * 3 // EXPERTS)
+    most = (most + 15) // 16 * 16
     mixed = convolve(mixer_in, conv_tail, conv_weight, conv_bias)
     partial_proj = jnp.dot(mixed, x_weight, preferred_element_type=jnp.float32)
-    projected = lax.psum(partial_proj.astype(jnp.bfloat16), "tensor").astype(jnp.float32)
+    projected = all_sum(partial_proj.astype(jnp.bfloat16), devices, 0).astype(jnp.float32)
     rank_part = projected[:, :RANK].astype(jnp.bfloat16)
     delta = jax.nn.softplus(
         jnp.dot(rank_part, dt_weight, preferred_element_type=jnp.float32) + dt_bias[None, :]
@@ -116,12 +400,12 @@
     )
     position = lax.axis_index("tensor")
     piece = readout
-    mixer_rows = lax.psum_scatter(
+    mixer_rows = scatter_sum(
         jnp.dot(piece, out_weight, preferred_element_type=jnp.float32).astype(jnp.bfloat16),
-        "tensor",
-        scatter_dimension=0,
-        tiled=True,
-    ).astype(jnp.float32)
+        devices,
+        8,
+        1,
+    )
     own_ids = lax.dynamic_slice_in_dim(expert_ids, position * own_count, own_count, 0)
     hidden_state = resid.astype(jnp.float32) + mixer_rows
     normed, route_weight = route_inputs(hidden_state, own_ids, norm_gain, router_weight)
@@ -130,18 +414,15 @@
         choose_real.astype(jnp.bfloat16), normed, preferred_element_type=jnp.float32
     ).astype(jnp.bfloat16)
     all_hidden = expert_hidden_rows(
-        lax.all_gather(packed, "tensor", axis=0, tiled=True), w_gate, w_up
+        gather(packed, devices, 4, 2), w_gate, w_up
     )
     piece = all_hidden
-    summed = lax.psum_scatter(
-        jnp.dot(piece, w_down, preferred_element_type=jnp.float32)
-        .astype(jnp.bfloat16)
-        .astype(jnp.float32)
-        .astype(jnp.bfloat16),
-        "tensor",
-        scatter_dimension=0,
-        tiled=True,
-    ).astype(jnp.float32)
+    summed = scatter_sum(
+        jnp.dot(piece, w_down, preferred_element_type=jnp.float32).astype(jnp.bfloat16),
+        devices,
+        4,
+        3,
+    )
     expert_rows = jnp.dot(coefficient.T, summed, precision=lax.Precision.HIGHEST)
     layer_out = (hidden_state + expert_rows).astype(jnp.bfloat16)
     return (layer_out, state_out)

time: 388 us -> 218 us (0.56); the launches traced: 382 us -> 218 us
  waiting for transfers between devices: 250 us -> 0 us
  Pallas kernels: 0 us -> 171 us
  blocking collectives: 48.5 us -> 0 us
  starting transfers between devices: 14.5 us -> 0 us
  between operations: 14.6 us -> 0.88 us
  local copies, waits for them, and re-layouts: 15.7 us -> 3.79 us
    pallas_call x0 -> x4, Pallas kernels: none -> 171 us  [the longest x2 106 us: scatter_sum(): pl.pallas_call(kernel, out_shape=jax.ShapeDtypeStruct((rows, width), jnp....]
    reduce_scatter x1 -> x0, waiting for transfers between devices: 103 us -> none  [per_device(): lax.psum_scatter(jnp.dot(piece, out_weight, preferred_element_type=jnp.fl...]
    psum x1 -> x0, waiting for transfers between devices: 93.3 us -> none  [per_device(): lax.psum(partial_proj.astype(jnp.bfloat16), 'tensor').astype(jnp.float32)]
    all_gather x1 -> x0, waiting for transfers between devices: 49 us -> none  [per_device(): lax.all_gather(packed, 'tensor', axis=0, tiled=True)]
    unnamed x1 -> x0, blocking collectives: 48.5 us -> none
    unnamed x4 -> x0, starting transfers between devices: 14.4 us -> none
    unnamed x32 -> x22, local copies, waits for them, and re-layouts: 12.5 us -> 0.86 us
    unnamed x7 -> x0, waiting for transfers between devices: 4.96 us -> none
  transfers between devices with their start and end apart: 7 -> 0, of which waited for: 4 -> 0; matrix products, arithmetic and copies ran while one was open for 1% -> 0% of each run, Pallas kernels for 0% -> 0%
where the time goes in v1:
time: 218 us
  Pallas kernels  171 us (78%)
  matrix products  30.3 us (14%)
  other arithmetic  11.7 us (5%)
  local copies, waits for them, and re-layouts  3.79 us (2%)
    pallas_call x2, Pallas kernels, scatter_sum(): pl.pallas_call(kernel, out_shape=jax.ShapeDtypeStruct((rows, width), jnp....  106 us
    pallas_call x1, Pallas kernels, gather(): pl.pallas_call(kernel, out_shape=jax.ShapeDtypeStruct((d2, d1, d0, rows,...  36 us
    pallas_call x1, Pallas kernels, all_sum(): pl.pallas_call(kernel, out_shape=jax.ShapeDtypeStruct((d2, d1, d0, rows,...  28.8 us
    dot_general x1, matrix products, per_device(): jnp.dot(piece, w_down, preferred_element_type=jnp.float32)  12.3 us
    dot_general x1, matrix products, expert_hidden_rows(): gated = jnp.dot(rows, w_gate, preferred_element_type=jnp.float32)  6.41 us
    dot_general x1, matrix products, per_device(): jnp.dot(piece, out_weight, preferred_element_type=jnp.float32)  5.58 us
    reduce_sum x1, other arithmetic, run_states(): jnp.sum(c_part[first:first + REQ][:, :, None] * state, axis=1)  4.97 us

profile of v1, /device:TPU:0, one launch (start us, length us, event | category | flops | bytes accessed | tf_op | source)
XLA Modules:
  0.0 217.8 jit_solution(17442359428744478999)
XLA Ops:
  0.6 0.0 copy-start
  0.6 0.8 constant_dynamic-slice_fusion
  1.5 0.8 fusion.67
  2.3 0.1 copy.30
  2.4 0.1 reduce-window.8
  2.4 0.1 reduce
  2.6 0.7 exponential_negate_fusion
  3.3 0.7 convert_element_type.136
  4.0 1.0 convert_element_type.113
  5.0 1.0 convert.23
  6.0 0.9 multiply_convert_fusion.1
  6.9 0.3 convolution_convert_fusion.3
  7.3 1.1 copy.29
  8.4 28.8 %all_sum.1 = bf16[4,2,2,32,544]{4,3,2,1,0:T(8,128)(2,1)} custom-call(bf16[4,2,2,32,544]{4,3,2,1,0:T(8,128)(2,1)} %bitcast.81), custom_call_target="tpu_custom_call" | custom-call | tf_op jit(solution)/shard_map/all_sum/pallas_call | solution.py:239
  37.2 1.6 compare_select_fusion
  38.8 0.1 convert_multiply_fusion.1
  38.9 0.1 bitcast_convert_fusion
  39.1 0.1 fusion.66
  39.2 0.8 copy-done.5
  40.0 5.0 %multiply_reduce_fusion.1 = (f32[128,256]{1,0:T(8,128)S(1)}, f32[128,256]{1,0:T(8,128)S(1)}, f32[128,256]{1,0:T(8,128)S(1)}, f32[128,256]{1,0:T(8,128)S(1)}, bf16[128,16,256]{2,1,0:T(8,128)(2,1)}) fusion(f32[128,16]{1,0:T(8,128)S(1)} %get-tuple-element.10, f32[128,256]{1,0:T(8,128)S(1)} %get-tuple-element.16, f32[128,256]{1,0:T(8,128)S(1)} %get-tuple-element.24, ...), kind=kLoop, calls=%fused_computation.7 | loop fusion | flops 13500416 | bytes 3751936 | tf_op jit(solution)/shard_map/reduce_sum | solution.py:326
  45.0 0.2 fusion.51
  45.2 5.6 %convolution_convert_fusion = bf16[512,8192]{1,0:T(8,128)(2,1)} fusion(bf16[256,8192]{1,0:T(8,128)(2,1)S(1)} %copy-done.3, bf16[128,256]{1,0:T(8,128)(2,1)S(1)} %get-tuple-element.21, bf16[128,256]{1,0:T(8,128)(2,1)S(1)} %get-tuple-element.22, bf16[128,256]{1,0:T(8,128)(2,1)S(1)} %get-tuple-element.20, bf16[128,256]{1,0:T(8,128)(2,1)S(1)} %get-tuple-element.19), kind=kOutput, calls=%fused_computation | convolution fusion | flops 2152726528 | bytes 12845056 | tf_op jit(solution)/shard_map/dot_general | solution.py:404
  50.8 63.8 %scatter_sum.2 = f32[32,8192]{1,0:T(8,128)} custom-call(bf16[4,2,2,32,8192]{4,3,2,1,0:T(8,128)(2,1)} %bitcast.79), custom_call_target="tpu_custom_call" | custom-call | tf_op jit(solution)/shard_map/scatter_sum/pallas_call | solution.py:266
  114.7 1.6 multiply_reduce_fusion.4
  116.2 0.2 multiply_convert_fusion
  116.5 0.2 fusion.68
  116.7 0.9 convolution_convert_fusion.2.x_ref
  117.7 36.0 %gather.1 = bf16[4,2,2,16,8192]{4,3,2,1,0:T(8,128)(2,1)} custom-call(bf16[16,8192]{1,0:T(8,128)(2,1)} %convolution_convert_fusion.2.x_ref), custom_call_target="tpu_custom_call" | custom-call | tf_op jit(solution)/shard_map/gather/pallas_call | solution.py:289
  153.7 6.4 %fusion.69 = f32[256,384]{1,0:T(8,128)S(1)} fusion(bf16[256,8192]{1,0:T(8,128)(2,1)} %bitcast.76, bf16[8192,384]{1,0:T(8,128)(2,1)} %param.35), kind=kOutput, calls=%fused_computation.126 | convolution fusion | flops 1610612736 | bytes 10878976 | tf_op jit(solution)/shard_map/dot_general | solution.py:358
  160.1 12.3 %convolution_convert_fusion.1 = bf16[256,8192]{1,0:T(8,128)(2,1)} fusion(bf16[384,8192]{1,0:T(8,128)(2,1)} %param.37, bf16[256,8192]{1,0:T(8,128)(2,1)} %bitcast.77, bf16[8192,384]{1,0:T(8,128)(2,1)} %param.36, f32[256,384]{1,0:T(8,128)S(1)} %fusion.69), kind=kOutput, calls=%fused_computation.1 | convolution fusion | flops 3223912448 | bytes 21364736 | tf_op jit(solution)/shard_map/dot_general | solution.py:421
  172.5 42.5 %scatter_sum.3 = f32[16,8192]{1,0:T(8,128)} custom-call(bf16[4,2,2,16,8192]{4,3,2,1,0:T(8,128)(2,1)} %bitcast.78), custom_call_target="tpu_custom_call" | custom-call | tf_op jit(solution)/shard_map/scatter_sum/pallas_call | solution.py:266
  214.9 2.9 %fusion = bf16[32,8192]{1,0:T(8,128)(2,1)} fusion(f32[16,8192]{1,0:T(8,128)} %scatter_sum.3, f32[32,8192]{1,0:T(8,128)S(1)} %copy-done.1, bf16[32,8192]{1,0:T(8,128)(2,1)S(1)} %copy-done.2, f32[32]{0:T(128)S(1)} %bitcast_select_fusion.1, s32[32]{0:T(128)S(1)} %fusion.62, pred[32]{0:T(512)(128)(4,1)S(1)} %broadcast_compare_fusion), kind=kOutput, calls=%fused_computation.3 | convolution fusion | flops 51381760 | bytes 2621728 | tf_op jit(solution)/shard_map/dot_general | solution.py:426
  (26 shorter events, 0.1 us)
Async XLA Ops:
  0.6 6.3 %copy-start = (bf16[256,544]{0,1:T(8,128)(2,1)S(1)}, bf16[256,544]{0,1:T(8,128)(2,1)}, u32[]{:S(2)}) copy-start(bf16[256,544]{0,1:T(8,128)(2,1)} %param.27) | copy-start | bytes 835588
  6.9 30.3 %copy-start.9 = (bf16[512,256]{1,0:T(8,128)(2,1)S(1)}, bf16[512,256]{1,0:T(8,128)(2,1)}, u32[]{:S(2)}) copy-start(bf16[512,256]{1,0:T(8,128)(2,1)} %param.28) | copy-start | bytes 786436
  6.9 30.3 %copy-start.10 = (f32[256]{0:T(256)S(1)}, f32[256]{0:T(256)}, u32[]{:S(2)}) copy-start(f32[256]{0:T(256)} %param.29) | copy-start | bytes 3076
  37.2 1.7 copy-start.4
  38.8 1.2 copy-start.5
  39.1 5.9 %copy-start.7 = (bf16[512,256]{1,0:T(8,128)(2,1)S(1)}, bf16[512,256]{1,0:T(8,128)(2,1)}, u32[]{:S(2)}) copy-start(bf16[512,256]{1,0:T(8,128)(2,1)} %param.20) | copy-start | bytes 786436
  40.0 5.0 %copy-start.8 = (f32[256]{0:T(256)S(1)}, f32[256]{0:T(256)}, u32[]{:S(2)}) copy-start(f32[256]{0:T(256)} %param.31) | copy-start | bytes 3076
  40.0 5.2 %copy-start.3 = (bf16[256,8192]{1,0:T(8,128)(2,1)S(1)}, bf16[256,8192]{1,0:T(8,128)(2,1)}, u32[]{:S(2)}) copy-start(bf16[256,8192]{1,0:T(8,128)(2,1)} %param.32) | copy-start | bytes 12582916
  50.8 63.8 %copy-start.2 = (bf16[32,8192]{1,0:T(8,128)(2,1)S(1)}, bf16[32,8192]{1,0:T(8,128)(2,1)}, u32[]{:S(2)}) copy-start(bf16[32,8192]{1,0:T(8,128)(2,1)} %param.23) | copy-start | bytes 1572868
  114.6 1.6 copy-start.1
  114.6 1.8 copy-start.6

commit v2 on v1

--- a/solution.py
+++ b/solution.py
@@ -72,7 +72,7 @@
     return value.astype(jnp.float32)
 
 
-def reduce_parts(place, chunks, x_ref, finish, recv0, recv1, recv2, sems):
+def reduce_parts(place, chunks, x_ref, produce, finish, recv0, recv1, recv2, sems):
     d2, d1, d0 = place.d2, place.d1, place.d0
     width = x_ref.shape[-1] // chunks
     copies = []
@@ -81,6 +81,7 @@
         return slice(None) if chunks == 1 else pl.ds(chunk * width, width)
 
     def start0(chunk):
+        produce(chunk, columns(chunk))
         return [
             send(
                 x_ref.at[:, :, place.digit(0, step), :, columns(chunk)],
@@ -140,20 +141,29 @@
         finish(chunk, columns(chunk), total)
         return []
 
-    flying = {}
-    for tick in range(chunks + 3):
-        for stage, run in enumerate((start0, start1, start2, last)):
-            chunk = tick - stage
-            if 0 <= chunk < chunks:
-                if stage:
-                    for copy in flying[stage - 1, chunk]:
-                        copy.wait_recv()
-                flying[stage, chunk] = run(chunk)
-                copies.extend(flying[stage, chunk])
+    def landed(group):
+        for copy in group:
+            copy.wait_recv()
+        copies.extend(group)
+
+    first, second = [], []
+    for chunk in range(chunks + 1):
+        if chunk < chunks:
+            first.append(start0(chunk))
+        if chunk > 0:
+            landed(first[chunk - 1])
+            second.append(start1(chunk - 1))
+    third = []
+    for chunk in range(chunks):
+        landed(second[chunk])
+        third.append(start2(chunk))
+    for chunk in range(chunks):
+        landed(third[chunk])
+        last(chunk)
     return copies
 
 
-def gather_parts(place, chunks, out_ref, sems):
+def gather_parts(place, chunks, out_ref, use, sems):
     d2, d1, d0 = place.d2, place.d1, place.d0
     width = out_ref.shape[-1] // chunks
     copies = []
@@ -168,29 +178,36 @@
             return out_ref.at[:, place.i1, place.i0, :, columns(chunk)]
         return out_ref.at[:, :, place.i0, :, columns(chunk)]
 
-    order = ((2, d2), (1, d1), (0, d0))
-    flying = {}
-    for tick in range(chunks + len(order)):
-        for spot in range(len(order) + 1):
-            chunk = tick - spot
-            if not 0 <= chunk < chunks:
-                continue
-            if spot:
-                for copy in flying[spot - 1, chunk]:
-                    copy.wait_recv()
-            if spot < len(order):
-                stage, radix = order[spot]
-                flying[spot, chunk] = [
-                    send(
-                        held(stage, chunk),
-                        held(stage, chunk),
-                        sems[2 * stage].at[chunk, step - 1],
-                        sems[2 * stage + 1].at[chunk, step - 1],
-                        place.device(stage, step),
-                    )
-                    for step in range(1, radix)
-                ]
-                copies.extend(flying[spot, chunk])
+    def start(stage, radix, chunk):
+        return [
+            send(
+                held(stage, chunk),
+                held(stage, chunk),
+                sems[2 * stage].at[chunk, step - 1],
+                sems[2 * stage + 1].at[chunk, step - 1],
+                place.device(stage, step),
+            )
+            for step in range(1, radix)
+        ]
+
+    def landed(group):
+        for copy in group:
+            copy.wait_recv()
+        copies.extend(group)
+
+    first = [start(2, d2, chunk) for chunk in range(chunks)]
+    second = []
+    for chunk in range(chunks):
+        landed(first[chunk])
+        second.append(start(1, d1, chunk))
+    third = []
+    for chunk in range(chunks + 1):
+        if chunk < chunks:
+            landed(second[chunk])
+            third.append(start(0, d0, chunk))
+        if chunk > 0:
+            landed(third[chunk - 1])
+            use(chunk - 1, columns(chunk - 1))
     return copies
 
 
@@ -211,10 +228,14 @@
     ]
 
 
-def params(number):
+def params(number, mebibytes):
     return pltpu.CompilerParams(
-        collective_id=number, has_side_effects=True, vmem_limit_bytes=56 * 1024 * 1024
+        collective_id=number, has_side_effects=True, vmem_limit_bytes=mebibytes * 1024 * 1024
     )
+
+
+def nothing(chunk, columns):
+    return None
 
 
 VMEM = pl.BlockSpec(memory_space=pltpu.VMEM)
@@ -231,8 +252,8 @@
         def finish(chunk, columns, total):
             out_ref[place.i2, place.i1, place.i0] = total.astype(out_ref.dtype)
 
-        copies = reduce_parts(place, 1, x_ref, finish, recv0, recv1, recv2, sems[:6])
-        copies += gather_parts(place, 1, out_ref, sems[6:])
+        copies = reduce_parts(place, 1, x_ref, nothing, finish, recv0, recv1, recv2, sems[:6])
+        copies += gather_parts(place, 1, out_ref, nothing, sems[6:])
         for copy in copies:
             copy.wait_send()
 
@@ -242,60 +263,119 @@
         in_specs=[VMEM],
         out_specs=VMEM,
         scratch_shapes=recv_shapes(devices, 1, rows, width) + sem_shapes(devices, 1) * 2,
-        compiler_params=params(number),
+        compiler_params=params(number, 8),
         name="all_sum",
     )(x.reshape(d2, d1, d0, rows, width))
     return out.reshape(x.shape)
 
 
-def scatter_sum(x, devices, chunks, number):
+def project_scatter(piece, weight, devices, chunks, number):
     d2, d1, d0 = radices(devices)
-    rows, width = x.shape[0] // devices, x.shape[1]
-
-    def kernel(x_ref, out_ref, recv0, recv1, recv2, *sems):
+    rows, width = piece.shape[0] // devices, weight.shape[1]
+
+    def kernel(piece_ref, weight_ref, out_ref, x_ref, recv0, recv1, recv2, *sems):
         place = Place(devices)
         place.barrier()
 
+        def produce(chunk, columns):
+            part = jnp.dot(
+                piece_ref[...], weight_ref[:, columns], preferred_element_type=jnp.float32
+            ).astype(jnp.bfloat16)
+            x_ref[:, :, :, :, columns] = part.reshape(d2, d1, d0, rows, width // chunks)
+
         def finish(chunk, columns, total):
             out_ref[:, columns] = total
 
-        copies = reduce_parts(place, chunks, x_ref, finish, recv0, recv1, recv2, sems)
+        copies = reduce_parts(place, chunks, x_ref, produce, finish, recv0, recv1, recv2, sems)
         for copy in copies:
             copy.wait_send()
 
     return pl.pallas_call(
         kernel,
         out_shape=jax.ShapeDtypeStruct((rows, width), jnp.float32),
-        in_specs=[VMEM],
+        in_specs=[VMEM, VMEM],
         out_specs=VMEM,
-        scratch_shapes=recv_shapes(devices, chunks, rows, width // chunks)
+        scratch_shapes=[pltpu.VMEM((d2, d1, d0, rows, width), jnp.bfloat16)]
+        + recv_shapes(devices, chunks, rows, width // chunks)
         + sem_shapes(devices, chunks),
-        compiler_params=params(number),
-        name="scatter_sum",
-    )(x.reshape(d2, d1, d0, rows, width))
-
-
-def gather(x, devices, chunks, number):
+        compiler_params=params(number, 40),
+        name="project_scatter",
+    )(piece, weight)
+
+
+def run_expert(packed, w_gate, w_up, w_down, devices, chunks, number):
     d2, d1, d0 = radices(devices)
-    rows, width = x.shape
-
-    def kernel(x_ref, out_ref, *sems):
+    rows, width = packed.shape
+    units = w_gate.shape[1]
+    tokens = devices * rows
+
+    def kernel(
+        packed_ref, gate_ref, up_ref, down_ref, out_ref,
+        all_ref, x_ref, both_ref, lower_ref, sum_ref, hidden_ref, load_sems, recv0, recv1, recv2, *sems
+    ):
+        loads = [
+            pltpu.make_async_copy(gate_ref, both_ref.at[:, pl.ds(0, units)], load_sems.at[0]),
+            pltpu.make_async_copy(up_ref, both_ref.at[:, pl.ds(units, units)], load_sems.at[1]),
+            pltpu.make_async_copy(down_ref, lower_ref, load_sems.at[2]),
+        ]
+        for load in loads:
+            load.start()
         place = Place(devices)
-        out_ref[place.i2, place.i1, place.i0] = x_ref[...]
+        all_ref[place.i2, place.i1, place.i0] = packed_ref[...]
         place.barrier()
-        for copy in gather_parts(place, chunks, out_ref, sems):
+
+        def use(chunk, columns):
+            if chunk == 0:
+                loads[0].wait()
+                loads[1].wait()
+            part = jnp.dot(
+                all_ref[:, :, :, :, columns].reshape(tokens, width // chunks),
+                both_ref[columns, :],
+                preferred_element_type=jnp.float32,
+            )
+            if chunk == 0:
+                sum_ref[...] = part
+            else:
+                sum_ref[...] += part
+
+        copies = gather_parts(place, chunks, all_ref, use, sems[:6])
+        hidden_ref[...] = (jax.nn.silu(sum_ref[:, :units]) * sum_ref[:, units:]).astype(jnp.bfloat16)
+        loads[2].wait()
+
+        def produce(chunk, columns):
+            part = jnp.dot(
+                hidden_ref[...], lower_ref[:, columns], preferred_element_type=jnp.float32
+            ).astype(jnp.bfloat16)
+            x_ref[:, :, :, :, columns] = part.reshape(d2, d1, d0, rows, width // chunks)
+
+        def finish(chunk, columns, total):
+            out_ref[:, columns] = total
+
+        copies += reduce_parts(
+            place, chunks, x_ref, produce, finish, recv0, recv1, recv2, sems[6:]
+        )
+        for copy in copies:
             copy.wait_send()
 
-    out = pl.pallas_call(
+    return pl.pallas_call(
         kernel,
-        out_shape=jax.ShapeDtypeStruct((d2, d1, d0, rows, width), x.dtype),
-        in_specs=[VMEM],
+        out_shape=jax.ShapeDtypeStruct((rows, width), jnp.float32),
+        in_specs=[VMEM] + [pl.BlockSpec(memory_space=pl.ANY)] * 3,
         out_specs=VMEM,
-        scratch_shapes=sem_shapes(devices, chunks),
-        compiler_params=params(number),
-        name="gather",
-    )(x)
-    return out.reshape(devices * rows, width)
+        scratch_shapes=[
+            pltpu.VMEM((d2, d1, d0, rows, width), jnp.bfloat16),
+            pltpu.VMEM((d2, d1, d0, rows, width), jnp.bfloat16),
+            pltpu.VMEM((width, 2 * units), jnp.bfloat16),
+            pltpu.VMEM((units, width), jnp.bfloat16),
+            pltpu.VMEM((tokens, 2 * units), jnp.float32),
+            pltpu.VMEM((tokens, units), jnp.bfloat16),
+            pltpu.SemaphoreType.DMA((3,)),
+        ]
+        + recv_shapes(devices, chunks, rows, width // chunks)
+        + sem_shapes(devices, chunks) * 2,
+        compiler_params=params(number, 56),
+        name="run_expert",
+    )(packed, w_gate, w_up, w_down)
 
 
 def convolve(mixer_in, conv_tail, conv_weight, conv_bias):
@@ -352,12 +432,6 @@
     choose = jnp.logical_and(member[None, :] > 0, ranked[None, :] == slots[:, None])
     choose_real = choose.astype(jnp.float32)
     return (choose_real, choose_real * route_weight[None, :])
-
-
-def expert_hidden_rows(rows, w_gate, w_up):
-    gated = jnp.dot(rows, w_gate, preferred_element_type=jnp.float32)
-    upward = jnp.dot(rows, w_up, preferred_element_type=jnp.float32)
-    return (jax.nn.silu(gated) * upward).astype(jnp.bfloat16)
 
 
 def per_device(
@@ -399,13 +473,7 @@
         mixed, gate_in, delta, b_part, c_part, ssm_state, decay_log, skip_gain
     )
     position = lax.axis_index("tensor")
-    piece = readout
-    mixer_rows = scatter_sum(
-        jnp.dot(piece, out_weight, preferred_element_type=jnp.float32).astype(jnp.bfloat16),
-        devices,
-        8,
-        1,
-    )
+    mixer_rows = project_scatter(readout, out_weight, devices, 16, 1)
     own_ids = lax.dynamic_slice_in_dim(expert_ids, position * own_count, own_count, 0)
     hidden_state = resid.astype(jnp.float32) + mixer_rows
     normed, route_weight = route_inputs(hidden_state, own_ids, norm_gain, router_weight)
@@ -413,16 +481,7 @@
     packed = jnp.dot(
         choose_real.astype(jnp.bfloat16), normed, preferred_element_type=jnp.float32
     ).astype(jnp.bfloat16)
-    all_hidden = expert_hidden_rows(
-        gather(packed, devices, 4, 2), w_gate, w_up
-    )
-    piece = all_hidden
-    summed = scatter_sum(
-        jnp.dot(piece, w_down, preferred_element_type=jnp.float32).astype(jnp.bfloat16),
-        devices,
-        4,
-        3,
-    )
+    summed = run_expert(packed, w_gate, w_up, w_down, devices, 8, 2)
     expert_rows = jnp.dot(coefficient.T, summed, precision=lax.Precision.HIGHEST)
     layer_out = (hidden_state + expert_rows).astype(jnp.bfloat16)
     return (layer_out, state_out)

time: 218 us -> 181 us (0.83)
  matrix products: 30.3 us -> 4.85 us
  Pallas kernels: 171 us -> 163 us
  other arithmetic: 11.7 us -> 9.01 us
    dot_general x3 -> x0, matrix products: 24.3 us -> none  [the longest x1 12.3 us: per_device(): jnp.dot(piece, w_down, preferred_element_type=jnp.float32)]
    pallas_call x3 -> x2, Pallas kernels: 142 us -> 137 us  [the longest x1 72.7 us: run_expert(): pl.pallas_call(kernel, out_shape=jax.ShapeDtypeStruct((rows, width), jnp....]
where the time goes in v2:
time: 181 us
  Pallas kernels  163 us (90%)
  other arithmetic  9.01 us (5%)
  matrix products  4.85 us (3%)
  local copies, waits for them, and re-layouts  2.98 us (2%)
    pallas_call x1, Pallas kernels, run_expert(): pl.pallas_call(kernel, out_shape=jax.ShapeDtypeStruct((rows, width), jnp....  72.7 us
    pallas_call x1, Pallas kernels, project_scatter(): pl.pallas_call(kernel, out_shape=jax.ShapeDtypeStruct((rows, width), jnp....  63.8 us
    pallas_call x1, Pallas kernels, all_sum(): pl.pallas_call(kernel, out_shape=jax.ShapeDtypeStruct((d2, d1, d0, rows,...  26.9 us
    reduce_sum x1, other arithmetic, run_states(): jnp.sum(c_part[first:first + REQ][:, :, None] * state, axis=1)  4.97 us

profile of v2, /device:TPU:0, one launch (start us, length us, event | category | flops | bytes accessed | tf_op | source)
XLA Modules:
  0.0 181.2 jit_solution(6918272421594028940)
XLA Ops:
  0.6 0.0 copy-start
  0.6 0.8 fusion.51
  1.5 1.0 convert.23
  2.5 1.0 convert_element_type.104
  3.4 0.9 multiply_convert_fusion.1
  4.4 0.0 copy-start.9
  4.4 0.0 copy-start.10
  4.4 0.3 convolution_convert_fusion.1
  4.7 0.3 copy.29
  5.0 26.9 %all_sum.1 = bf16[4,2,2,32,544]{4,3,2,1,0:T(8,128)(2,1)S(1)} custom-call(bf16[4,2,2,32,544]{4,3,2,1,0:T(8,128)(2,1)S(1)} %bitcast.67), custom_call_target="tpu_custom_call" | custom-call | tf_op jit(solution)/shard_map/all_sum/pallas_call | solution.py:260
  32.0 0.5 compare_select_fusion
  32.5 0.0 copy-start.7
  32.5 0.0 copy-start.3
  32.5 0.1 convert_multiply_fusion.1
  32.6 0.1 bitcast_convert_fusion
  32.8 0.1 fusion.50
  32.9 0.3 copy-done.7
  33.2 0.5 copy-done.3
  33.7 5.0 %multiply_reduce_fusion.1 = (f32[128,256]{1,0:T(8,128)S(1)}, f32[128,256]{1,0:T(8,128)S(1)}, f32[128,256]{1,0:T(8,128)S(1)}, f32[128,256]{1,0:T(8,128)S(1)}, bf16[128,16,256]{2,1,0:T(8,128)(2,1)}) fusion(f32[128,16]{1,0:T(8,128)S(1)} %get-tuple-element.10, f32[128,256]{1,0:T(8,128)S(1)} %get-tuple-element.16, f32[128,256]{1,0:T(8,128)S(1)} %get-tuple-element.24, ...), kind=kLoop, calls=%fused_computation.5 | loop fusion | flops 13500416 | bytes 3751936 | tf_op jit(solution)/shard_map/reduce_sum | solution.py:406
  38.7 0.2 fusion.37
  39.0 0.0 copy-start.2
  39.0 63.8 %project_scatter.1 = f32[32,8192]{1,0:T(8,128)S(1)} custom-call(bf16[512,256]{1,0:T(8,128)(2,1)S(1)} %pad_maximum_fusion.1.piece_ref, bf16[256,8192]{1,0:T(8,128)(2,1)S(1)} %copy-done.1), custom_call_target="tpu_custom_call" | custom-call | tf_op jit(solution)/shard_map/project_scatter/pallas_call | solution.py:293
  102.8 0.2 multiply_reduce_fusion.4
  103.0 0.2 multiply_convert_fusion
  103.3 0.8 constant_dynamic-slice_fusion
  104.0 0.1 copy.30
  104.1 0.1 reduce-window.8
  104.2 0.1 reduce
  104.3 0.9 convolution_convert_fusion.packed_ref
  105.2 72.7 %run_expert.1 = f32[16,8192]{1,0:T(8,128)} custom-call(bf16[16,8192]{1,0:T(8,128)(2,1)} %convolution_convert_fusion.packed_ref, bf16[8192,384]{1,0:T(8,128)(2,1)} %gate_ref.1, bf16[8192,384]{1,0:T(8,128)(2,1)} %up_ref.1, bf16[384,8192]{1,0:T(8,128)(2,1)} %down_ref.1), custom_call_target="tpu_custom_call" | custom-call | tf_op jit(solution)/shard_map/run_expert/pallas_call | solution.py:360
  178.0 0.2 fusion.52
  178.3 2.9 %fusion = bf16[32,8192]{1,0:T(8,128)(2,1)} fusion(f32[16,8192]{1,0:T(8,128)} %run_expert.1, f32[32,8192]{1,0:T(8,128)S(1)} %project_scatter.1, bf16[32,8192]{1,0:T(8,128)(2,1)S(1)} %copy-done.2, f32[32]{0:T(128)S(1)} %bitcast_select_fusion.1, s32[32]{0:T(128)S(1)} %fusion.48, pred[32]{0:T(512)(128)(4,1)S(1)} %broadcast_compare_fusion), kind=kOutput, calls=%fused_computation.1 | convolution fusion | flops 51381760 | bytes 2621728 | tf_op jit(solution)/shard_map/dot_general | solution.py:485
  (23 shorter events, 0.1 us)
Async XLA Ops:
  0.6 3.8 %copy-start = (bf16[256,544]{0,1:T(8,128)(2,1)S(1)}, bf16[256,544]{0,1:T(8,128)(2,1)}, u32[]{:S(2)}) copy-start(bf16[256,544]{0,1:T(8,128)(2,1)} %param.27) | copy-start | bytes 835588
  4.4 27.6 %copy-start.9 = (bf16[512,256]{1,0:T(8,128)(2,1)S(1)}, bf16[512,256]{1,0:T(8,128)(2,1)}, u32[]{:S(2)}) copy-start(bf16[512,256]{1,0:T(8,128)(2,1)} %param.28) | copy-start | bytes 786436
  4.4 27.6 %copy-start.10 = (f32[256]{0:T(256)S(1)}, f32[256]{0:T(256)}, u32[]{:S(2)}) copy-start(f32[256]{0:T(256)} %param.29) | copy-start | bytes 3076
  32.5 0.7 copy-start.7
  32.5 1.2 copy-start.3
  32.8 5.9 %copy-start.5 = (bf16[512,256]{1,0:T(8,128)(2,1)S(1)}, bf16[512,256]{1,0:T(8,128)(2,1)}, u32[]{:S(2)}) copy-start(bf16[512,256]{1,0:T(8,128)(2,1)} %param.20) | copy-start | bytes 786436
  33.7 5.0 %copy-start.8 = (f32[256]{0:T(256)S(1)}, f32[256]{0:T(256)}, u32[]{:S(2)}) copy-start(f32[256]{0:T(256)} %param.31) | copy-start | bytes 3076
  33.7 5.2 %copy-start.1 = (bf16[256,8192]{1,0:T(8,128)(2,1)S(1)}, bf16[256,8192]{1,0:T(8,128)(2,1)}, u32[]{:S(2)}) copy-start(bf16[256,8192]{1,0:T(8,128)(2,1)} %weight_ref.1) | copy-start | bytes 12582916
  39.0 63.8 %copy-start.2 = (bf16[32,8192]{1,0:T(8,128)(2,1)S(1)}, bf16[32,8192]{1,0:T(8,128)(2,1)}, u32[]{:S(2)}) copy-start(bf16[32,8192]{1,0:T(8,128)(2,1)} %param.23) | copy-start | bytes 1572868
  39.0 64.1 %copy-start.6 = (bf16[8192]{0:T(1024)(128)(2,1)S(1)}, bf16[8192]{0:T(1024)(128)(2,1)}, u32[]{:S(2)}) copy-start(bf16[8192]{0:T(1024)(128)(2,1)} %param.33) | copy-start | bytes 49156
  105.2 72.7 %copy-start.4 = (bf16[8192,16]{0,1:T(8,128)(2,1)S(1)}, bf16[8192,16]{0,1:T(8,128)(2,1)}, u32[]{:S(2)}) copy-start(bf16[8192,16]{0,1:T(8,128)(2,1)} %param.34) | copy-start | bytes 786436

commit v3 on v2

v3 whole, which is shorter than its diff:
```python
import itertools

import jax
import jax.numpy as jnp
from jax import lax
from jax.experimental import pallas as pl
from jax.experimental.pallas import tpu as pltpu
from jax.sharding import PartitionSpec as P

RANK = 512
STATE = 16
CONV = 4
EXPERTS = 16
TOPK = 2
STEPS = 4
REQ = 128


EPSILON = 1e-06
MESH = pl.DeviceIdType.MESH


def radices(devices, widest):
    chips = devices // 2
    digits = [2]
    if chips % 4:
        digits.append(chips)
        return digits
    while chips > 1:
        radix = 2 if chips == 8 else min(widest, chips)
        digits.append(radix)
        chips //= radix
    return digits


class Place:
    def __init__(self, digits):
        self.digits = digits
        self.group = lax.axis_index("groups")
        rest = lax.axis_index("tensor")
        self.own = []
        for radix in digits:
            self.own.append(lax.rem(rest, radix))
            rest = rest // radix

    def digit(self, stage, step):
        return lax.rem(self.own[stage] + step, self.digits[stage])

    def device(self, stage, step):
        index = 0
        for place in reversed(range(len(self.digits))):
            now = self.digit(place, step) if place == stage else self.own[place]
            index = index * self.digits[place] + now
        return (self.group, index)

    def block(self):
        return tuple(reversed(self.own))

    def barrier(self):
        semaphore = pltpu.get_barrier_semaphore()
        count = 0
        for stage, radix in enumerate(self.digits):
            for step in range(1, radix):
                pl.semaphore_signal(
                    semaphore, inc=1, device_id=self.device(stage, step), device_id_type=MESH
                )
                count += 1
        pl.semaphore_wait(semaphore, count)


def send(source, target, send_sem, recv_sem, device):
    copy = pltpu.make_async_remote_copy(
        src_ref=source,
        dst_ref=target,
        send_sem=send_sem,
        recv_sem=recv_sem,
        device_id=device,
        device_id_type=MESH,
    )
    copy.start()
    return copy


def real(value):
    return value.astype(jnp.float32)


def wait_landed(group):
    for copy in group:
        copy.wait_recv()


def reduce_parts(place, chunks, x_ref, produce, finish, recvs, sems):
    digits = place.digits
    stages = len(digits)
    width = x_ref.shape[-1] // chunks

    def columns(chunk):
        return slice(None) if chunks == 1 else pl.ds(chunk * width, width)

    def held(stage, chunk, index):
        if stage == 0:
            return x_ref.at[index + (slice(None), columns(chunk))]
        return recvs[stage - 1].at[(chunk, 0) + index]

    def start(stage, chunk):
        outer = (slice(None),) * (stages - 1 - stage)
        return [
            send(
                held(stage, chunk, outer + (place.digit(stage, step),)),
                recvs[stage].at[chunk, step - 1],
                sems[2 * stage].at[chunk, step - 1],
                sems[2 * stage + 1].at[chunk, step - 1],
                place.device(stage, step),
            )
            for step in range(1, digits[stage])
        ]

    def add(stage, chunk):
        recv = recvs[stage]
        for outer in itertools.product(*map(range, reversed(digits[stage + 1 :]))):
            total = real(held(stage, chunk, outer + (place.own[stage],))[...])
            for step in range(1, digits[stage]):
                total = total + real(recv[(chunk, step - 1) + outer])
            if stage == stages - 1:
                finish(chunk, columns(chunk), total)
            else:
                recv[(chunk, 0) + outer] = total.astype(recv.dtype)

    copies, flying, following = [], [], []
    for chunk in range(chunks + 1):
        if chunk < chunks:
            produce(chunk, columns(chunk))
            flying.append(start(0, chunk))
        if chunk > 0:
            wait_landed(flying[chunk - 1])
            add(0, chunk - 1)
            following.append(start(1, chunk - 1))
    for stage in range(1, stages):
        copies += flying
        flying, following = following, []
        for chunk in range(chunks):
            wait_landed(flying[chunk])
            add(stage, chunk)
            if stage + 1 < stages:
                following.append(start(stage + 1, chunk))
    copies += flying
    return [copy for group in copies for copy in group]


def gather_parts(place, chunks, out_ref, use, sems):
    stages = len(place.digits)
    width = out_ref.shape[-1] // chunks

    def columns(chunk):
        return slice(None) if chunks == 1 else pl.ds(chunk * width, width)

    def start(stage, chunk):
        index = (slice(None),) * (stages - 1 - stage) + place.block()[stages - 1 - stage :]
        held = out_ref.at[index + (slice(None), columns(chunk))]
        return [
            send(
                held,
                held,
                sems[2 * stage].at[chunk, step - 1],
                sems[2 * stage + 1].at[chunk, step - 1],
                place.device(stage, step),
            )
            for step in range(1, place.digits[stage])
        ]

    copies = []
    flying = [start(stages - 1, chunk) for chunk in range(chunks)]
    for stage in reversed(range(1, stages - 1)):
        copies += flying
        following = []
        for chunk in range(chunks):
            wait_landed(flying[chunk])
            following.append(start(stage, chunk))
        flying = following
    copies += flying
    last = []
    for chunk in range(chunks + 1):
        if chunk < chunks:
            wait_landed(flying[chunk])
            last.append(start(0, chunk))
        if chunk > 0:
            wait_landed(last[chunk - 1])
            use(chunk - 1, columns(chunk - 1))
    copies += last
    return [copy for group in copies for copy in group]


def sem_shapes(digits, chunks):
    shapes = []
    for radix in digits:
        shapes += [pltpu.SemaphoreType.DMA((chunks, radix - 1))] * 2
    return shapes


def recv_shapes(digits, chunks, rows, width):
    return [
        pltpu.VMEM(
            (chunks, radix - 1) + tuple(reversed(digits[stage + 1 :])) + (rows, width), jnp.bfloat16
        )
        for stage, radix in enumerate(digits)
    ]


def params(number, mebibytes):
    return pltpu.CompilerParams(
        collective_id=number, has_side_effects=True, vmem_limit_bytes=mebibytes * 1024 * 1024
    )


def nothing(chunk, columns):
    return None


VMEM = pl.BlockSpec(memory_space=pltpu.VMEM)


def all_sum(x, devices, number):
    digits = radices(devices, 4)
    count = len(digits)
    shape = tuple(reversed(digits))
    rows, width = x.shape[0] // devices, x.shape[1]

    def kernel(x_ref, out_ref, *scratch):
        recvs, sems = scratch[:count], scratch[count:]
        place = Place(digits)
        place.barrier()

        def finish(chunk, columns, total):
            out_ref[place.block()] = total.astype(out_ref.dtype)

        copies = reduce_parts(place, 1, x_ref, nothing, finish, recvs, sems[: 2 * count])
        copies += gather_parts(place, 1, out_ref, nothing, sems[2 * count :])
        for copy in copies:
            copy.wait_send()

    out = pl.pallas_call(
        kernel,
        out_shape=jax.ShapeDtypeStruct(shape + (rows, width), jnp.bfloat16),
        in_specs=[VMEM],
        out_specs=VMEM,
        scratch_shapes=recv_shapes(digits, 1, rows, width) + sem_shapes(digits, 1) * 2,
        compiler_params=params(number, 8),
        name="all_sum",
    )(x.reshape(shape + (rows, width)))
    return out.reshape(x.shape)


def project_scatter(piece, weight, devices, chunks, number):
    digits = radices(devices, 2)
    count = len(digits)
    shape = tuple(reversed(digits))
    rows, width = piece.shape[0] // devices, weight.shape[1]

    def kernel(piece_ref, weight_ref, out_ref, x_ref, *scratch):
        recvs, sems = scratch[:count], scratch[count:]
        place = Place(digits)
        place.barrier()

        def produce(chunk, columns):
            part = jnp.dot(
                piece_ref[...], weight_ref[:, columns], preferred_element_type=jnp.float32
            ).astype(jnp.bfloat16)
            x_ref[(slice(None),) * (count + 1) + (columns,)] = part.reshape(
                shape + (rows, width // chunks)
            )

        def finish(chunk, columns, total):
            out_ref[:, columns] = total

        copies = reduce_parts(place, chunks, x_ref, produce, finish, recvs, sems)
        for copy in copies:
            copy.wait_send()

    return pl.pallas_call(
        kernel,
        out_shape=jax.ShapeDtypeStruct((rows, width), jnp.float32),
        in_specs=[VMEM, VMEM],
        out_specs=VMEM,
        scratch_shapes=[pltpu.VMEM(shape + (rows, width), jnp.bfloat16)]
        + recv_shapes(digits, chunks, rows, width // chunks)
        + sem_shapes(digits, chunks),
        compiler_params=params(number, 40),
        name="project_scatter",
    )(piece, weight)


def run_expert(packed, w_gate, w_up, w_down, devices, chunks, number):
    digits = radices(devices, 2)
    count = len(digits)
    shape = tuple(reversed(digits))
    rows, width = packed.shape
    units = w_gate.shape[1]
    tokens = devices * rows

    def kernel(
        packed_ref, gate_ref, up_ref, down_ref, out_ref,
        all_ref, x_ref, both_ref, lower_ref, sum_ref, hidden_ref, load_sems, *scratch
    ):
        recvs, sems = scratch[:count], scratch[count:]
        loads = [
            pltpu.make_async_copy(gate_ref, both_ref.at[:, pl.ds(0, units)], load_sems.at[0]),
            pltpu.make_async_copy(up_ref, both_ref.at[:, pl.ds(units, units)], load_sems.at[1]),
            pltpu.make_async_copy(down_ref, lower_ref, load_sems.at[2]),
        ]
        for load in loads:
            load.start()
        place = Place(digits)
        all_ref[place.block()] = packed_ref[...]
        place.barrier()

        def use(chunk, columns):
            if chunk == 0:
                loads[0].wait()
                loads[1].wait()
            part = jnp.dot(
                all_ref[(slice(None),) * (count + 1) + (columns,)].reshape(tokens, width // chunks),
                both_ref[columns, :],
                preferred_element_type=jnp.float32,
            )
            if chunk == 0:
                sum_ref[...] = part
            else:
                sum_ref[...] += part

        copies = gather_parts(place, chunks, all_ref, use, sems[: 2 * count])
        hidden_ref[...] = (jax.nn.silu(sum_ref[:, :units]) * sum_ref[:, units:]).astype(jnp.bfloat16)
        loads[2].wait()

        def produce(chunk, columns):
            part = jnp.dot(
                hidden_ref[...], lower_ref[:, columns], preferred_element_type=jnp.float32
            ).astype(jnp.bfloat16)
            x_ref[(slice(None),) * (count + 1) + (columns,)] = part.reshape(
                shape + (rows, width // chunks)
            )

        def finish(chunk, columns, total):
            out_ref[:, columns] = total

        copies += reduce_parts(
            place, chunks, x_ref, produce, finish, recvs, sems[2 * count :]
        )
        for copy in copies:
            copy.wait_send()

    return pl.pallas_call(
        kernel,
        out_shape=jax.ShapeDtypeStruct((rows, width), jnp.float32),
        in_specs=[VMEM] + [pl.BlockSpec(memory_space=pl.ANY)] * 3,
        out_specs=VMEM,
        scratch_shapes=[
            pltpu.VMEM(shape + (rows, width), jnp.bfloat16),
            pltpu.VMEM(shape + (rows, width), jnp.bfloat16),
            pltpu.VMEM((width, 2 * units), jnp.bfloat16),
            pltpu.VMEM((units, width), jnp.bfloat16),
            pltpu.VMEM((tokens, 2 * units), jnp.float32),
            pltpu.VMEM((tokens, units), jnp.bfloat16),
            pltpu.SemaphoreType.DMA((3,)),
        ]
        + recv_shapes(digits, chunks, rows, width // chunks)
        + sem_shapes(digits, chunks) * 2,
        compiler_params=params(number, 56),
        name="run_expert",
    )(packed, w_gate, w_up, w_down)


def convolve(mixer_in, conv_tail, conv_weight, conv_bias):
    width = mixer_in.shape[1]
    inputs = mixer_in.reshape(STEPS, REQ, width).astype(jnp.float32)
    history = jnp.concatenate([conv_tail.astype(jnp.float32), inputs], axis=0)
    kernel = conv_weight.astype(jnp.float32)
    summed = conv_bias[None, None, :] + kernel[0] * history[0:STEPS]
    for offset in range(1, CONV):
        summed = summed + kernel[offset] * history[offset : offset + STEPS]
    return jax.nn.silu(summed).astype(jnp.bfloat16).reshape(STEPS * REQ, width)


def run_states(mixed, gate_in, delta, b_part, c_part, ssm_state, decay_log, skip_gain):
    rate = -jnp.exp(decay_log)
    state = ssm_state.astype(jnp.float32)
    results = []
    for position in range(STEPS):
        first = position * REQ
        step_delta = delta[first : first + REQ]
        step_input = mixed[first : first + REQ].astype(jnp.float32)
        decay = jnp.exp(step_delta[:, None, :] * rate[None, :, :])
        state = (
            decay * state
            + (step_delta * step_input)[:, None, :] * b_part[first : first + REQ][:, :, None]
        )
        reading = (
            jnp.sum(c_part[first : first + REQ][:, :, None] * state, axis=1)
            + skip_gain[None, :] * step_input
        )
        results.append(reading * jax.nn.silu(gate_in[first : first + REQ].astype(jnp.float32)))
    return (jnp.concatenate(results, axis=0).astype(jnp.bfloat16), state.astype(jnp.bfloat16))


def route_inputs(hidden_state, expert_ids, norm_gain, router_weight):
    scale = lax.rsqrt(jnp.mean(hidden_state * hidden_state, axis=1, keepdims=True) + EPSILON)
    normed = (hidden_state * scale * norm_gain.astype(jnp.float32)[None, :]).astype(jnp.bfloat16)
    logits = jnp.dot(normed, router_weight, preferred_element_type=jnp.float32)
    labels = jnp.arange(logits.shape[1], dtype=jnp.int32)
    onehot = expert_ids[:, :, None] == labels[None, None, :]
    picked = jnp.sum(jnp.where(onehot, logits[:, None, :], 0.0), axis=2)
    weight_first = jax.nn.sigmoid(picked[:, 0] - picked[:, 1])
    weight_second = jax.nn.sigmoid(picked[:, 1] - picked[:, 0])
    route_weight = jnp.where(
        expert_ids[:, 0] == 0, weight_first, jnp.where(expert_ids[:, 1] == 0, weight_second, 0.0)
    )
    return (normed, route_weight)


def slot_matrix(own_ids, route_weight, most):
    member = jnp.logical_or(own_ids[:, 0] == 0, own_ids[:, 1] == 0).astype(jnp.int32)
    ranked = jnp.cumsum(member, dtype=jnp.int32) - member
    slots = jnp.arange(most, dtype=jnp.int32)
    choose = jnp.logical_and(member[None, :] > 0, ranked[None, :] == slots[:, None])
    choose_real = choose.astype(jnp.float32)
    return (choose_real, choose_real * route_weight[None, :])


def per_device(
    mixer_in,
    gate_in,
    conv_tail,
    ssm_state,
    resid,
    expert_ids,
    conv_weight,
    conv_bias,
    x_weight,
    dt_weight,
    dt_bias,
    decay_log,
    skip_gain,
    out_weight,
    norm_gain,
    router_weight,
    w_gate,
    w_up,
    w_down,
):
    devices = lax.axis_size("tensor")
    tokens_total = mixer_in.shape[0]
    own_count = tokens_total // devices
    most = max(2, own_count * TOPK * 3 // EXPERTS)
    most = (most + 15) // 16 * 16
    mixed = convolve(mixer_in, conv_tail, conv_weight, conv_bias)
    partial_proj = jnp.dot(mixed, x_weight, preferred_element_type=jnp.float32)
    projected = all_sum(partial_proj.astype(jnp.bfloat16), devices, 0).astype(jnp.float32)
    rank_part = projected[:, :RANK].astype(jnp.bfloat16)
    delta = jax.nn.softplus(
        jnp.dot(rank_part, dt_weight, preferred_element_type=jnp.float32) + dt_bias[None, :]
    )
    b_part = projected[:, RANK : RANK + STATE]
    c_part = projected[:, RANK + STATE :]
    readout, state_out = run_states(
        mixed, gate_in, delta, b_part, c_part, ssm_state, decay_log, skip_gain
    )
    position = lax.axis_index("tensor")
    mixer_rows = project_scatter(readout, out_weight, devices, 16, 1)
    own_ids = lax.dynamic_slice_in_dim(expert_ids, position * own_count, own_count, 0)
    hidden_state = resid.astype(jnp.float32) + mixer_rows
    normed, route_weight = route_inputs(hidden_state, own_ids, norm_gain, router_weight)
    choose_real, coefficient = slot_matrix(own_ids, route_weight, most)
    packed = jnp.dot(
        choose_real.astype(jnp.bfloat16), normed, preferred_element_type=jnp.float32
    ).astype(jnp.bfloat16)
    summed = run_expert(packed, w_gate, w_up, w_down, devices, 8, 2)
    expert_rows = jnp.dot(coefficient.T, summed, precision=lax.Precision.HIGHEST)
    layer_out = (hidden_state + expert_rows).astype(jnp.bfloat16)
    return (layer_out, state_out)


def solution(mesh):
    return jax.shard_map(
        per_device,
        mesh=mesh,
        in_specs=(
            P("groups", "tensor"),
            P("groups", "tensor"),
            P(None, "groups", "tensor"),
            P("groups", None, "tensor"),
            P(("groups", "tensor"), None),
            P("groups", None),
            P(None, "tensor"),
            P("tensor"),
            P("tensor", None),
            P(None, "tensor"),
            P("tensor"),
            P(None, "tensor"),
            P("tensor"),
            P("tensor", None),
            P(),
            P(),
            P(None, "tensor"),
            P(None, "tensor"),
            P("tensor", None),
        ),
        out_specs=(P(("groups", "tensor"), None), P("groups", None, "tensor")),
        check_vma=False,
    )
```

time: 181 us -> 203 us (1.12)
  Pallas kernels: 163 us -> 185 us
    pallas_call x1, Pallas kernels: 63.8 us -> 77.4 us  [project_scatter(): pl.pallas_call(kernel, out_shape=jax.ShapeDtypeStruct((rows, width), jnp....]
    pallas_call x1, Pallas kernels: 72.7 us -> 80.4 us  [run_expert(): pl.pallas_call(kernel, out_shape=jax.ShapeDtypeStruct((rows, width), jnp....]
where the time goes in v3:
time: 203 us; the launch traced here: 202 us
  Pallas kernels  185 us (91%)
  other arithmetic  9.01 us (4%)
  matrix products  4.85 us (2%)
  local copies, waits for them, and re-layouts  2.98 us (1%)
    pallas_call x1, Pallas kernels, run_expert(): pl.pallas_call(kernel, out_shape=jax.ShapeDtypeStruct((rows, width), jnp....  80.4 us
    pallas_call x1, Pallas kernels, project_scatter(): pl.pallas_call(kernel, out_shape=jax.ShapeDtypeStruct((rows, width), jnp....  77.4 us
    pallas_call x1, Pallas kernels, all_sum(): pl.pallas_call(kernel, out_shape=jax.ShapeDtypeStruct(shape + (rows, widt...  26.9 us
    reduce_sum x1, other arithmetic, run_states(): jnp.sum(c_part[first:first + REQ][:, :, None] * state, axis=1)  4.97 us

profile of v3, /device:TPU:0, one launch (start us, length us, event | category | flops | bytes accessed | tf_op | source)
XLA Modules:
  0.0 202.4 jit_solution(9873235607804169180)
XLA Ops:
  0.6 0.0 copy-start
  0.6 0.8 fusion.51
  1.5 1.0 convert.23
  2.5 1.0 convert_element_type.104
  3.4 0.9 multiply_convert_fusion.1
  4.4 0.0 copy-start.9
  4.4 0.0 copy-start.10
  4.4 0.3 convolution_convert_fusion.1
  4.7 0.3 copy.29
  5.0 26.9 %all_sum.1 = bf16[4,2,2,32,544]{4,3,2,1,0:T(8,128)(2,1)S(1)} custom-call(bf16[4,2,2,32,544]{4,3,2,1,0:T(8,128)(2,1)S(1)} %bitcast.67), custom_call_target="tpu_custom_call" | custom-call | tf_op jit(solution)/shard_map/all_sum/pallas_call | solution.py:242
  32.0 0.5 compare_select_fusion
  32.5 0.1 convert_multiply_fusion.1
  32.6 0.1 bitcast_convert_fusion
  32.7 0.0 copy-start.5
  32.7 0.1 fusion.50
  32.9 0.3 copy-done.7
  33.2 0.5 copy-done.3
  33.7 5.0 %multiply_reduce_fusion.1 = (f32[128,256]{1,0:T(8,128)S(1)}, f32[128,256]{1,0:T(8,128)S(1)}, f32[128,256]{1,0:T(8,128)S(1)}, f32[128,256]{1,0:T(8,128)S(1)}, bf16[128,16,256]{2,1,0:T(8,128)(2,1)}) fusion(f32[128,16]{1,0:T(8,128)S(1)} %get-tuple-element.10, f32[128,256]{1,0:T(8,128)S(1)} %get-tuple-element.16, f32[128,256]{1,0:T(8,128)S(1)} %get-tuple-element.24, ...), kind=kLoop, calls=%fused_computation.5 | loop fusion | flops 13500416 | bytes 3751936 | tf_op jit(solution)/shard_map/reduce_sum | solution.py:398
  38.7 0.2 fusion.37
  38.9 0.0 copy-start.2
  38.9 0.0 copy-start.6
  38.9 77.4 %project_scatter.1 = f32[32,8192]{1,0:T(8,128)S(1)} custom-call(bf16[512,256]{1,0:T(8,128)(2,1)S(1)} %pad_maximum_fusion.1.piece_ref, bf16[256,8192]{1,0:T(8,128)(2,1)S(1)} %copy-done.1), custom_call_target="tpu_custom_call" | custom-call | tf_op jit(solution)/shard_map/project_scatter/pallas_call | solution.py:280
  116.3 0.2 multiply_reduce_fusion.4
  116.6 0.2 multiply_convert_fusion
  116.8 0.8 constant_dynamic-slice_fusion
  117.6 0.1 copy.30
  117.7 0.1 reduce-window.8
  117.7 0.1 reduce
  117.9 0.9 convolution_convert_fusion.packed_ref
  118.8 80.4 %run_expert.1 = f32[16,8192]{1,0:T(8,128)} custom-call(bf16[16,8192]{1,0:T(8,128)(2,1)} %convolution_convert_fusion.packed_ref, bf16[8192,384]{1,0:T(8,128)(2,1)} %gate_ref.1, bf16[8192,384]{1,0:T(8,128)(2,1)} %up_ref.1, bf16[384,8192]{1,0:T(8,128)(2,1)} %down_ref.1), custom_call_target="tpu_custom_call" | custom-call | tf_op jit(solution)/shard_map/run_expert/pallas_call | solution.py:352
  199.2 0.2 fusion.52
  199.5 2.9 %fusion = bf16[32,8192]{1,0:T(8,128)(2,1)} fusion(f32[16,8192]{1,0:T(8,128)} %run_expert.1, f32[32,8192]{1,0:T(8,128)S(1)} %project_scatter.1, bf16[32,8192]{1,0:T(8,128)(2,1)S(1)} %copy-done.2, f32[32]{0:T(128)S(1)} %bitcast_select_fusion.1, s32[32]{0:T(128)S(1)} %fusion.48, pred[32]{0:T(512)(128)(4,1)S(1)} %broadcast_compare_fusion), kind=kOutput, calls=%fused_computation.1 | convolution fusion | flops 51381760 | bytes 2621728 | tf_op jit(solution)/shard_map/dot_general | solution.py:477
  (23 shorter events, 0.1 us)
Async XLA Ops:
  0.6 3.8 %copy-start = (bf16[256,544]{0,1:T(8,128)(2,1)S(1)}, bf16[256,544]{0,1:T(8,128)(2,1)}, u32[]{:S(2)}) copy-start(bf16[256,544]{0,1:T(8,128)(2,1)} %param.27) | copy-start | bytes 835588
  4.4 27.6 %copy-start.9 = (bf16[512,256]{1,0:T(8,128)(2,1)S(1)}, bf16[512,256]{1,0:T(8,128)(2,1)}, u32[]{:S(2)}) copy-start(bf16[512,256]{1,0:T(8,128)(2,1)} %param.28) | copy-start | bytes 786436
  4.4 27.6 %copy-start.10 = (f32[256]{0:T(256)S(1)}, f32[256]{0:T(256)}, u32[]{:S(2)}) copy-start(f32[256]{0:T(256)} %param.29) | copy-start | bytes 3076
  32.4 0.7 copy-start.7
  32.5 1.2 copy-start.3
  32.7 5.9 %copy-start.5 = (bf16[512,256]{1,0:T(8,128)(2,1)S(1)}, bf16[512,256]{1,0:T(8,128)(2,1)}, u32[]{:S(2)}) copy-start(bf16[512,256]{1,0:T(8,128)(2,1)} %param.20) | copy-start | bytes 786436
  33.7 5.0 %copy-start.8 = (f32[256]{0:T(256)S(1)}, f32[256]{0:T(256)}, u32[]{:S(2)}) copy-start(f32[256]{0:T(256)} %param.31) | copy-start | bytes 3076
  33.7 5.2 %copy-start.1 = (bf16[256,8192]{1,0:T(8,128)(2,1)S(1)}, bf16[256,8192]{1,0:T(8,128)(2,1)}, u32[]{:S(2)}) copy-start(bf16[256,8192]{1,0:T(8,128)(2,1)} %weight_ref.1) | copy-start | bytes 12582916
  38.9 77.4 %copy-start.2 = (bf16[32,8192]{1,0:T(8,128)(2,1)S(1)}, bf16[32,8192]{1,0:T(8,128)(2,1)}, u32[]{:S(2)}) copy-start(bf16[32,8192]{1,0:T(8,128)(2,1)} %param.23) | copy-start | bytes 1572868
  38.9 77.6 %copy-start.6 = (bf16[8192]{0:T(1024)(128)(2,1)S(1)}, bf16[8192]{0:T(1024)(128)(2,1)}, u32[]{:S(2)}) copy-start(bf16[8192]{0:T(1024)(128)(2,1)} %param.33) | copy-start | bytes 49156
  118.8 80.4 %copy-start.4 = (bf16[8192,16]{0,1:T(8,128)(2,1)S(1)}, bf16[8192,16]{0,1:T(8,128)(2,1)}, u32[]{:S(2)}) copy-start(bf16[8192,16]{0,1:T(8,128)(2,1)} %param.34) | copy-start | bytes 786436

commit v4 on v3

--- a/solution.py
+++ b/solution.py
@@ -127,25 +127,24 @@
             else:
                 recv[(chunk, 0) + outer] = total.astype(recv.dtype)
 
-    copies, flying, following = [], [], []
+    flying = [[] for _ in range(stages)]
     for chunk in range(chunks + 1):
         if chunk < chunks:
             produce(chunk, columns(chunk))
-            flying.append(start(0, chunk))
+            flying[0].append(start(0, chunk))
         if chunk > 0:
-            wait_landed(flying[chunk - 1])
+            wait_landed(flying[0][chunk - 1])
             add(0, chunk - 1)
-            following.append(start(1, chunk - 1))
-    for stage in range(1, stages):
-        copies += flying
-        flying, following = following, []
-        for chunk in range(chunks):
-            wait_landed(flying[chunk])
-            add(stage, chunk)
-            if stage + 1 < stages:
-                following.append(start(stage + 1, chunk))
-    copies += flying
-    return [copy for group in copies for copy in group]
+            flying[1].append(start(1, chunk - 1))
+    for tick in range(chunks + 2 * (stages - 2)):
+        for stage in range(1, stages):
+            chunk = tick - 2 * (stage - 1)
+            if 0 <= chunk < chunks:
+                wait_landed(flying[stage][chunk])
+                add(stage, chunk)
+                if stage + 1 < stages:
+                    flying[stage + 1].append(start(stage + 1, chunk))
+    return [copy for groups in flying for group in groups for copy in group]
 
 
 def gather_parts(place, chunks, out_ref, use, sems):
@@ -169,26 +168,19 @@
             for step in range(1, place.digits[stage])
         ]
 
-    copies = []
-    flying = [start(stages - 1, chunk) for chunk in range(chunks)]
-    for stage in reversed(range(1, stages - 1)):
-        copies += flying
-        following = []
-        for chunk in range(chunks):
-            wait_landed(flying[chunk])
-            following.append(start(stage, chunk))
-        flying = following
-    copies += flying
-    last = []
-    for chunk in range(chunks + 1):
-        if chunk < chunks:
-            wait_landed(flying[chunk])
-            last.append(start(0, chunk))
-        if chunk > 0:
-            wait_landed(last[chunk - 1])
-            use(chunk - 1, columns(chunk - 1))
-    copies += last
-    return [copy for group in copies for copy in group]
+    flying = [[] for _ in range(stages)]
+    flying[stages - 1] = [start(stages - 1, chunk) for chunk in range(chunks)]
+    for tick in range(chunks + stages + 1):
+        for spot in range(stages):
+            stage = stages - 2 - spot
+            chunk = tick - spot - (1 if stage == 0 else 2 if stage < 0 else 0)
+            if 0 <= chunk < chunks:
+                wait_landed(flying[stage + 1][chunk])
+                if stage < 0:
+                    use(chunk, columns(chunk))
+                else:
+                    flying[stage].append(start(stage, chunk))
+    return [copy for groups in flying for group in groups for copy in group]
 
 
 def sem_shapes(digits, chunks):

time: 203 us -> 179 us (0.88)
  Pallas kernels: 185 us -> 161 us
    pallas_call x1, Pallas kernels: 77.4 us -> 59.6 us  [project_scatter(): pl.pallas_call(kernel, out_shape=jax.ShapeDtypeStruct((rows, width), jnp....]
    pallas_call x1, Pallas kernels: 80.4 us -> 74.7 us  [run_expert(): pl.pallas_call(kernel, out_shape=jax.ShapeDtypeStruct((rows, width), jnp....]
where the time goes in v4:
time: 179 us
  Pallas kernels  161 us (90%)
  other arithmetic  9.01 us (5%)
  matrix products  4.85 us (3%)
  local copies, waits for them, and re-layouts  2.98 us (2%)
    pallas_call x1, Pallas kernels, run_expert(): pl.pallas_call(kernel, out_shape=jax.ShapeDtypeStruct((rows, width), jnp....  74.7 us
    pallas_call x1, Pallas kernels, project_scatter(): pl.pallas_call(kernel, out_shape=jax.ShapeDtypeStruct((rows, width), jnp....  59.6 us
    pallas_call x1, Pallas kernels, all_sum(): pl.pallas_call(kernel, out_shape=jax.ShapeDtypeStruct(shape + (rows, widt...  26.9 us
    reduce_sum x1, other arithmetic, run_states(): jnp.sum(c_part[first:first + REQ][:, :, None] * state, axis=1)  4.97 us

profile of v4, /device:TPU:0, one launch (start us, length us, event | category | flops | bytes accessed | tf_op | source)
XLA Modules:
  0.0 178.9 jit_solution(317228867977235384)
XLA Ops:
  0.6 0.0 copy-start
  0.6 0.8 fusion.51
  1.5 1.0 convert.23
  2.5 1.0 convert_element_type.104
  3.4 0.9 multiply_convert_fusion.1
  4.4 0.0 copy-start.9
  4.4 0.0 copy-start.10
  4.4 0.3 convolution_convert_fusion.1
  4.7 0.3 copy.29
  5.0 26.9 %all_sum.1 = bf16[4,2,2,32,544]{4,3,2,1,0:T(8,128)(2,1)S(1)} custom-call(bf16[4,2,2,32,544]{4,3,2,1,0:T(8,128)(2,1)S(1)} %bitcast.67), custom_call_target="tpu_custom_call" | custom-call | tf_op jit(solution)/shard_map/all_sum/pallas_call | solution.py:234
  32.0 0.5 compare_select_fusion
  32.5 0.0 copy-start.7
  32.5 0.0 copy-start.3
  32.5 0.1 convert_multiply_fusion.1
  32.6 0.1 bitcast_convert_fusion
  32.7 0.1 fusion.50
  32.9 0.3 copy-done.7
  33.2 0.5 copy-done.3
  33.7 5.0 %multiply_reduce_fusion.1 = (f32[128,256]{1,0:T(8,128)S(1)}, f32[128,256]{1,0:T(8,128)S(1)}, f32[128,256]{1,0:T(8,128)S(1)}, f32[128,256]{1,0:T(8,128)S(1)}, bf16[128,16,256]{2,1,0:T(8,128)(2,1)}) fusion(f32[128,16]{1,0:T(8,128)S(1)} %get-tuple-element.10, f32[128,256]{1,0:T(8,128)S(1)} %get-tuple-element.16, f32[128,256]{1,0:T(8,128)S(1)} %get-tuple-element.24, ...), kind=kLoop, calls=%fused_computation.5 | loop fusion | flops 13500416 | bytes 3751936 | tf_op jit(solution)/shard_map/reduce_sum | solution.py:390
  38.7 0.2 fusion.37
  38.9 0.0 copy-start.2
  39.0 59.6 %project_scatter.1 = f32[32,8192]{1,0:T(8,128)S(1)} custom-call(bf16[512,256]{1,0:T(8,128)(2,1)S(1)} %pad_maximum_fusion.1.piece_ref, bf16[256,8192]{1,0:T(8,128)(2,1)S(1)} %copy-done.1), custom_call_target="tpu_custom_call" | custom-call | tf_op jit(solution)/shard_map/project_scatter/pallas_call | solution.py:272
  98.5 0.2 multiply_reduce_fusion.4
  98.8 0.2 multiply_convert_fusion
  99.0 0.8 constant_dynamic-slice_fusion
  99.8 0.1 copy.30
  99.9 0.1 reduce-window.8
  99.9 0.1 reduce
  100.1 0.9 convolution_convert_fusion.packed_ref
  101.0 74.7 %run_expert.1 = f32[16,8192]{1,0:T(8,128)} custom-call(bf16[16,8192]{1,0:T(8,128)(2,1)} %convolution_convert_fusion.packed_ref, bf16[8192,384]{1,0:T(8,128)(2,1)} %gate_ref.1, bf16[8192,384]{1,0:T(8,128)(2,1)} %up_ref.1, bf16[384,8192]{1,0:T(8,128)(2,1)} %down_ref.1), custom_call_target="tpu_custom_call" | custom-call | tf_op jit(solution)/shard_map/run_expert/pallas_call | solution.py:344
  175.7 0.2 fusion.52
  176.0 2.9 %fusion = bf16[32,8192]{1,0:T(8,128)(2,1)} fusion(f32[16,8192]{1,0:T(8,128)} %run_expert.1, f32[32,8192]{1,0:T(8,128)S(1)} %project_scatter.1, bf16[32,8192]{1,0:T(8,128)(2,1)S(1)} %copy-done.2, f32[32]{0:T(128)S(1)} %bitcast_select_fusion.1, s32[32]{0:T(128)S(1)} %fusion.48, pred[32]{0:T(512)(128)(4,1)S(1)} %broadcast_compare_fusion), kind=kOutput, calls=%fused_computation.1 | convolution fusion | flops 51381760 | bytes 2621728 | tf_op jit(solution)/shard_map/dot_general | solution.py:469
  (23 shorter events, 0.1 us)
Async XLA Ops:
  0.6 3.8 %copy-start = (bf16[256,544]{0,1:T(8,128)(2,1)S(1)}, bf16[256,544]{0,1:T(8,128)(2,1)}, u32[]{:S(2)}) copy-start(bf16[256,544]{0,1:T(8,128)(2,1)} %param.27) | copy-start | bytes 835588
  4.4 27.6 %copy-start.9 = (bf16[512,256]{1,0:T(8,128)(2,1)S(1)}, bf16[512,256]{1,0:T(8,128)(2,1)}, u32[]{:S(2)}) copy-start(bf16[512,256]{1,0:T(8,128)(2,1)} %param.28) | copy-start | bytes 786436
  4.4 27.6 %copy-start.10 = (f32[256]{0:T(256)S(1)}, f32[256]{0:T(256)}, u32[]{:S(2)}) copy-start(f32[256]{0:T(256)} %param.29) | copy-start | bytes 3076
  32.5 0.7 copy-start.7
  32.5 1.2 copy-start.3
  32.7 5.9 %copy-start.5 = (bf16[512,256]{1,0:T(8,128)(2,1)S(1)}, bf16[512,256]{1,0:T(8,128)(2,1)}, u32[]{:S(2)}) copy-start(bf16[512,256]{1,0:T(8,128)(2,1)} %param.20) | copy-start | bytes 786436
  33.7 5.0 %copy-start.8 = (f32[256]{0:T(256)S(1)}, f32[256]{0:T(256)}, u32[]{:S(2)}) copy-start(f32[256]{0:T(256)} %param.31) | copy-start | bytes 3076
  33.7 5.2 %copy-start.1 = (bf16[256,8192]{1,0:T(8,128)(2,1)S(1)}, bf16[256,8192]{1,0:T(8,128)(2,1)}, u32[]{:S(2)}) copy-start(bf16[256,8192]{1,0:T(8,128)(2,1)} %weight_ref.1) | copy-start | bytes 12582916
  38.9 59.6 %copy-start.2 = (bf16[32,8192]{1,0:T(8,128)(2,1)S(1)}, bf16[32,8192]{1,0:T(8,128)(2,1)}, u32[]{:S(2)}) copy-start(bf16[32,8192]{1,0:T(8,128)(2,1)} %param.23) | copy-start | bytes 1572868
  38.9 59.8 %copy-start.6 = (bf16[8192]{0:T(1024)(128)(2,1)S(1)}, bf16[8192]{0:T(1024)(128)(2,1)}, u32[]{:S(2)}) copy-start(bf16[8192]{0:T(1024)(128)(2,1)} %param.33) | copy-start | bytes 49156
  101.0 74.7 %copy-start.4 = (bf16[8192,16]{0,1:T(8,128)(2,1)S(1)}, bf16[8192,16]{0,1:T(8,128)(2,1)}, u32[]{:S(2)}) copy-start(bf16[8192,16]{0,1:T(8,128)(2,1)} %param.34) | copy-start | bytes 786436
